TPU v7x, 512 devices: a whole 4x8x8 slice. The times are simulated.
512 devices in a mesh: seg: 64 (over z, y_lo, core), dom: 8 (over x, y_hi).
Axes of the slice: x: 4, y: 8 (y_hi: 2, y_lo: 4; y = y_hi * 4 + y_lo), z: 8, core: 2. Of those that a mesh axis runs over, the one named last changes fastest.
Arguments:
- tangent: float32 [64, 2, 2048, 512], P('seg', None, 'dom'), may hold values from -6 to 6
- base_swirl: float32 [64, 2048, 512], P('seg', 'dom'), may hold values from -0.5 to 0.5
- metric: float32 [2048, 512], P('dom'), may hold values from 0.05 to 0.2
- stiffness: float32 [8, 8], replicated
- face_slot: int32 [2048, 6], P('dom'), may hold values from 0 to 831, as said below
- corners: int32 [2048, 8], P('dom'), may hold values from 0 to 511
- coarse_inverse: float32 [512, 512], replicated
- phase_angle: float32 [1], replicated, may hold values from -3.140625 to 3.140625
Outputs:
- mismatch: float32 [64, 2, 2048, 512], P('seg', None, 'dom')
Inputs may be any that keep to these rules, and one draw needn't show every extreme that they name: `face_slot`: within each slab of 256 elements along dom, every slot from 64 to 767 holds exactly two of the slab's faces, and every slot below 64 or from 768 on holds exactly one.
All inputs are finite; a program needn't handle non-finite values.
Results may differ from a plain program's by a relative error of at most 0.0001.
Values sent between devices are 32-bit elements; how exact they have to be, the bound alone decides.
No kernel may reach another device: no remote copies, remote signals or barrier semaphores. Data moves between devices by JAX's collectives and lax.ppermute only.
A program may use at most 128 MiB of HBM per device.

v0:
```python
import jax
import jax.numpy as jnp
import numpy as np
from jax import lax
from jax.experimental import pallas as pl
from jax.experimental.pallas import tpu as pltpu
from jax.sharding import PartitionSpec as P

F32 = jnp.float32
BF16 = jnp.bfloat16
NP = 8
NODES = 512
ELEMS = 256
FACES = 6
PLANE = 64
SHARED = 64
HALO = 2 * SHARED
INNER_TOP = 768
MSG1 = 88
MSG2 = 72
FACE_CORNERS = (
    (0, 1, 2, 3),
    (4, 5, 6, 7),
    (0, 1, 4, 5),
    (2, 3, 6, 7),
    (0, 2, 4, 6),
    (1, 3, 5, 7),
)


def tables():
    points = -np.cos(np.pi * np.arange(NP) / (NP - 1))
    linear = np.stack([(1.0 - points) / 2.0, (1.0 + points) / 2.0])
    basis = (
        linear[:, None, None, :, None, None]
        * linear[None, :, None, None, :, None]
        * linear[None, None, :, None, None, :]
    ).reshape(8, NODES)
    flat = (linear[:, None, :, None] * linear[None, :, None, :]).reshape(4, PLANE)
    pair = np.zeros((8, 2 * PLANE))
    pair[:4, :PLANE] = flat
    pair[4:, PLANE:] = flat
    node = np.arange(NODES).reshape(NP, NP, NP)
    faces = [node[0], node[-1], node[:, 0], node[:, -1], node[:, :, 0], node[:, :, -1]]
    chosen = np.concatenate([f.reshape(-1) for f in faces])
    select = (np.arange(NODES)[:, None] == chosen[None, :]).astype(np.float32)
    return basis.astype(np.float32), pair.astype(np.float32), select


def dot(a, b):
    return lax.dot_general(a, b, (((1,), (0,)), ((), ())), preferred_element_type=F32)


def dot_nt(a, b):
    return lax.dot_general(a, b, (((1,), (1,)), ((), ())), preferred_element_type=F32)


def dot_tn(a, b):
    return lax.dot_general(a, b, (((0,), (0,)), ((), ())), preferred_element_type=F32)


def split(x):
    high = x.astype(BF16)
    return high, (x - high.astype(F32)).astype(BF16)


def stacked(x):
    high = x.astype(BF16).astype(F32)
    return jnp.concatenate([high, x - high], axis=0).astype(BF16)


def hot(mask):
    return jnp.where(mask, F32(1.0), F32(0.0)).astype(BF16)


def iota(shape, dim):
    return lax.broadcasted_iota(jnp.int32, shape, dim)


def slot_rows(fs_ref):
    rows = fs_ref[...].astype(F32)
    return [rows[f : f + 1, :] for f in range(FACES)]


def slot_columns(fs_ref):
    rows = fs_ref[...].astype(F32)
    columns = jnp.concatenate([rows, rows[:2]], axis=0).T
    return [columns[:, f : f + 1] for f in range(FACES)]


def corner_parts(cor_ref):
    ids = cor_ref[...]
    return (ids >> 7).astype(F32), (ids & 127).astype(F32)


def row_of(parts):
    return jnp.concatenate([parts[k : k + 1, :] for k in range(parts.shape[0])], axis=1)


def stiff_matrix(sti):
    rest = sti - sti.astype(BF16).astype(F32)
    low = rest - rest.astype(BF16).astype(F32)
    parts = jnp.concatenate(
        [sti.astype(BF16).astype(F32), rest.astype(BF16).astype(F32), low, jnp.zeros((8, 8), F32)], axis=0
    ).astype(BF16)
    row, col = iota((NODES, 8), 0), iota((NODES, 8), 1)
    col32, lane = iota((32, NODES), 0), iota((32, NODES), 1)
    from_n = iota((NODES, 1), 0)
    to_n = iota((1, NODES), 1)
    total = jnp.zeros((NODES, NODES), F32)
    for shift, keep in ((6, 63), (3, 455), (0, 504)):
        source = hot(((row >> shift) & 7) == col)
        target = hot(((lane >> shift) & 7) == (col32 & 7))
        spread = dot_nt(source, parts)
        spread = dot(spread.astype(BF16), target)
        same = (from_n & keep) == (to_n & keep)
        total = total + jnp.where(same, spread, F32(0.0))
    return total


def advance(state, bh, bl, metric, swirl):
    high, low = split(state)
    stiff = dot(high, bh) + dot(low, bh) + dot(high, bl)
    re, im = state[:ELEMS], state[ELEMS:]
    new_re = re - metric * stiff[:ELEMS] - swirl * im
    new_im = im - metric * stiff[ELEMS:] + swirl * re
    return jnp.concatenate([new_re, new_im], axis=0)


def face_block(fh, fl, f):
    lanes = slice(f * PLANE, (f + 1) * PLANE)
    return jnp.concatenate(
        [fh[:ELEMS, lanes], fh[ELEMS:, lanes], fl[:ELEMS, lanes], fl[ELEMS:, lanes]], axis=1
    ).astype(BF16)


def to_elements(blocks):
    re = jnp.concatenate([b[:, :PLANE] for b in blocks], axis=1)
    im = jnp.concatenate([b[:, PLANE:] for b in blocks], axis=1)
    return jnp.concatenate([re, im], axis=0)


def multiplicity():
    n = iota((1, NODES), 1)
    total = jnp.zeros((1, NODES), F32)
    for shift in (6, 3, 0):
        at = (n >> shift) & 7
        total = total + jnp.where((at == 0) | (at == 7), F32(1.0), F32(0.0))
    return total


def deposit(values, high_ids, low_hot):
    vh = (iota((8, 1), 0) & 3).astype(F32)
    chosen = jnp.where(high_ids == vh, values, F32(0.0))
    both = dot_nt(stacked(chosen), low_hot)
    return both[:8] + both[8:]


def eight(re, im):
    return jnp.where(iota((8, 1), 0) < 4, re, im)


def coarse_of(settled, basis, cvh_row, bm):
    sh, sl = split(settled)
    scaled = basis * F32(1.0 / NODES)
    two = stacked(scaled)
    first = dot_nt(two, sh)
    second = dot_nt(two, sl)
    r = first[:8] + first[8:] + second[:8]
    re = row_of(r[:, :ELEMS])
    im = row_of(r[:, ELEMS:])
    return deposit(eight(re, im), cvh_row, bm)


def face_restricted(yh, yl, pair):
    scaled = pair * F32(0.5 / NODES)
    two = stacked(scaled)
    first = dot_nt(two, yh.astype(BF16))
    second = dot_nt(two, yl.astype(BF16))
    return first[:8] + first[8:] + second[:8]


def solve(coarse, kh, kl):
    rows = [jnp.concatenate([coarse[4 * c + h : 4 * c + h + 1] for h in range(4)], axis=1) for c in range(2)]
    flat = jnp.concatenate(rows, axis=0)
    high = flat.astype(BF16).astype(F32)
    packed = jnp.concatenate([high, flat - high, jnp.zeros((12, NODES), F32)], axis=0).astype(BF16)
    first = dot_nt(packed, kh)
    second = dot_nt(packed, kl)
    solved = first[0:2] + first[2:4] + second[0:2]
    return jnp.concatenate(
        [solved[c : c + 1, 128 * h : 128 * (h + 1)] for c in range(2) for h in range(4)], axis=0
    )


def correction(solved, basis, cvh_row, bm):
    both = dot(stacked(solved), bm)
    spread = both[:8] + both[8:]
    vh = (iota((8, 1), 0) & 3).astype(F32)
    spread = jnp.where(cvh_row == vh, spread, F32(0.0))
    lines = []
    for c in range(2):
        line = jnp.sum(spread[4 * c : 4 * c + 4], axis=0, keepdims=True)
        lines.append(jnp.concatenate([line[:, ELEMS * k : ELEMS * (k + 1)] for k in range(8)], axis=0))
    by_corner = jnp.concatenate(lines, axis=1)
    high = by_corner.astype(BF16).astype(F32)
    left = jnp.concatenate([high, by_corner - high, high, jnp.zeros((8, NODES), F32)], axis=0)
    bas_high = basis.astype(BF16).astype(F32)
    right = jnp.concatenate([bas_high, bas_high, basis - bas_high, jnp.zeros((8, NODES), F32)], axis=0)
    return dot_tn(left.astype(BF16), right.astype(BF16))


def shared_target_column():
    s = iota((HALO, 1), 0)
    return jnp.where(s < SHARED, s, s + (INNER_TOP - SHARED)).astype(F32)


def shared_target_row():
    s = iota((1, HALO), 1)
    return jnp.where(s < SHARED, s, s + (INNER_TOP - SHARED)).astype(F32)


def halo_part(columns, arrived, select):
    high, low = split(arrived)
    both = jnp.concatenate([high.astype(F32), low.astype(F32)], axis=1).astype(BF16)
    target = shared_target_row()
    blocks_h, blocks_l = [], []
    for f in range(FACES):
        got = dot(hot(columns[f] == target), both)
        blocks_h.append(got[:, :HALO])
        blocks_l.append(got[:, HALO:])
    return dot_nt(to_elements(blocks_h).astype(BF16), select) + dot_nt(
        to_elements(blocks_l).astype(BF16), select
    )


def local_settle(advanced, select, pairing, q_ref, out_ref):
    ah, al = split(advanced)
    fh = dot(ah, select)
    fl = dot(al, select)
    for f in range(FACES):
        q_ref[f * ELEMS : (f + 1) * ELEMS, :] = face_block(fh, fl, f)
    blocks = []
    for f in range(FACES):
        got = dot(pairing(f), q_ref[...])
        blocks.append(got[:, :HALO] + got[:, HALO:])
    gathered = to_elements(blocks)
    gh, gl = split(gathered)
    lift = dot_nt(gh, select) + dot_nt(gl, select)
    out_ref[...] = advanced * (F32(1.0) - multiplicity()) + F32(0.5) * lift


def send_rows(msg_ref, me, head, rows):
    count = head.shape[0]
    up, down = rows[:SHARED], rows[SHARED:]
    after = lax.rem(me + 1, 8)
    for j in range(8):
        msg_ref[j, 0:count, :] = head
        msg_ref[j, count : count + SHARED, :] = jnp.where(after == j, down, up)


def first_kernel(
    tan_ref, swl_ref, met_ref, sti_ref, fs_ref, cor_ref, sel_ref, bas_ref, pair_ref,
    out_ref, msg_ref, p_ref, bm_ref, bh_ref, bl_ref, q_ref,
):
    me = lax.axis_index("dom")
    bh, bl = split(stiff_matrix(sti_ref[...]))
    bh_ref[...] = bh
    bl_ref[...] = bl
    rows = slot_rows(fs_ref)
    row = jnp.concatenate(rows, axis=1)
    columns = slot_columns(fs_ref)
    for f in range(FACES):
        p_ref[f * ELEMS : (f + 1) * ELEMS, :] = hot(columns[f] == row)
    cvh, cvl = corner_parts(cor_ref)
    cvh_row = row_of(cvh)
    bm_ref[...] = hot(row_of(cvl) == iota((128, 1), 0).astype(F32))
    basis = bas_ref[...]

    advanced = advance(tan_ref[...], bh_ref[...], bl_ref[...], met_ref[...], swl_ref[...])
    local_settle(
        advanced, sel_ref[...], lambda f: p_ref[f * ELEMS : (f + 1) * ELEMS, :], q_ref, out_ref
    )
    coarse = coarse_of(out_ref[...], basis, cvh_row, bm_ref[...])
    shared = hot(shared_target_column() == row)
    y = dot(shared, q_ref[...])
    yh, yl = y[:, :HALO], y[:, HALO:]
    rf = face_restricted(yh, yl, pair_ref[...])
    face_ids = jnp.concatenate(
        [
            jnp.concatenate(
                [part[FACE_CORNERS[f][r] : FACE_CORNERS[f][r] + 1, :] for f in range(FACES)], axis=1
            )
            for part in (cvh, cvl)
            for r in range(4)
        ]
        * 2,
        axis=0,
    ).astype(BF16)
    ids = dot_nt(face_ids, shared)[:8]
    send_rows(msg_ref, me, jnp.concatenate([coarse, rf, ids], axis=0), yh + yl)


def second_kernel(
    s1_ref, got_ref, p_ref, bm_ref, bh_ref, bl_ref, swl_ref, met_ref, fs_ref, cor_ref, sel_ref, bas_ref,
    pair_ref, inv_ref,
    out_ref, msg_ref, q_ref,
):
    me = lax.axis_index("dom")
    before, after = lax.rem(me + 7, 8), lax.rem(me + 1, 8)
    kh, kl = split(inv_ref[...])
    basis = bas_ref[...]
    select = sel_ref[...]
    columns = slot_columns(fs_ref)
    row = jnp.concatenate(slot_rows(fs_ref), axis=1)
    cvh, _ = corner_parts(cor_ref)
    cvh_row = row_of(cvh)
    which = iota((128, 1), 0).astype(F32)

    coarse = got_ref[0, 0:8, :]
    for j in range(1, 8):
        coarse = coarse + got_ref[j, 0:8, :]
    rf = jnp.concatenate([got_ref[j, 8:16, :] for j in range(8)], axis=1)
    ids = jnp.concatenate([got_ref[j, 16:24, :] for j in range(8)], axis=1)
    from_left = jnp.concatenate([ids[:, 1024 - SHARED :], ids[:, : 1024 - SHARED]], axis=1)
    from_right = jnp.concatenate([ids[:, SHARED:], ids[:, :SHARED]], axis=1)
    partner = jnp.where((iota((1, 1024), 1) & SHARED) == 0, from_left, from_right)
    for r in range(4):
        low_hot = hot(partner[4 + r : 5 + r, :] == which)
        coarse = coarse + deposit(
            eight(rf[r : r + 1, :], rf[4 + r : 5 + r, :]), partner[r : r + 1, :], low_hot
        )
    solved = solve(coarse, kh, kl)

    arrived = jnp.concatenate([got_ref[before, 24:MSG1, :], got_ref[after, 24:MSG1, :]], axis=0)
    current = (
        s1_ref[...]
        + F32(0.5) * halo_part(columns, arrived, select)
        - correction(solved, basis, cvh_row, bm_ref[...])
    )
    advanced = advance(current, bh_ref[...], bl_ref[...], met_ref[...], swl_ref[...])
    local_settle(advanced, select, lambda f: p_ref[f * ELEMS : (f + 1) * ELEMS, :], q_ref, out_ref)
    coarse = coarse_of(out_ref[...], basis, cvh_row, bm_ref[...])
    shared = hot(shared_target_column() == row)
    y = dot(shared, q_ref[...])
    yh, yl = y[:, :HALO], y[:, HALO:]
    rf = face_restricted(yh, yl, pair_ref[...])
    mine = jnp.concatenate([got_ref[before, 16:24, SHARED:], got_ref[after, 16:24, :SHARED]], axis=1)
    for r in range(4):
        low_hot = hot(mine[4 + r : 5 + r, :] == which)
        coarse = coarse + deposit(eight(rf[r : r + 1, :], rf[4 + r : 5 + r, :]), mine[r : r + 1, :], low_hot)
    send_rows(msg_ref, me, coarse, yh + yl)


def pack_kernel(got_ref, inv_ref, out_ref):
    me = lax.axis_index("dom")
    kh, kl = split(inv_ref[...])
    coarse = got_ref[0, 0:8, :]
    for j in range(1, 8):
        coarse = coarse + got_ref[j, 0:8, :]
    out_ref[0:8, :] = solve(coarse, kh, kl)
    out_ref[8 : 8 + SHARED, :] = got_ref[lax.rem(me + 7, 8), 8:MSG2, :]
    out_ref[8 + SHARED :, :] = got_ref[lax.rem(me + 1, 8), 8:MSG2, :]


def last_kernel(tan_ref, s2_ref, small_ref, bm_ref, fs_ref, cor_ref, sel_ref, bas_ref, ang_ref, out_ref):
    cvh, _ = corner_parts(cor_ref)
    state = (
        s2_ref[...]
        + F32(0.5) * halo_part(slot_columns(fs_ref), small_ref[8:, :], sel_ref[...])
        - correction(small_ref[0:8, :], bas_ref[...], row_of(cvh), bm_ref[...])
    )
    angle = jnp.where(lax.axis_index("seg") == 0, ang_ref[0], F32(0.0))
    angles = jnp.full((1, NODES), angle, F32)
    cosine, sine = jnp.cos(angles), jnp.sin(angles)
    re, im = state[:ELEMS], state[ELEMS:]
    out_ref[0:ELEMS, :] = tan_ref[0:ELEMS, :] - (cosine * re - sine * im)
    out_ref[ELEMS:, :] = tan_ref[ELEMS:, :] - (sine * re + cosine * im)


VMEM = pl.BlockSpec(memory_space=pltpu.VMEM)
SMEM = pl.BlockSpec(memory_space=pltpu.SMEM)


def call(body, outs, scratch, ins, flops, specs=None, limit=40):
    size = sum(int(np.prod(o.shape)) * o.dtype.itemsize for o in outs)
    size += sum(int(np.prod(a.shape)) * a.dtype.itemsize for a in ins)
    return pl.pallas_call(
        body,
        out_shape=outs,
        in_specs=specs or [VMEM] * len(ins),
        out_specs=[VMEM] * len(outs),
        scratch_shapes=scratch,
        compiler_params=pltpu.CompilerParams(vmem_limit_bytes=limit * 1024 * 1024),
        cost_estimate=pl.CostEstimate(flops=flops, bytes_accessed=size, transcendentals=0),
    )(*ins)


def shards(tangent, base_swirl, metric, stiffness, face_slot, corners, coarse_inverse, phase_angle):
    basis, pair, select = tables()
    basis, pair, select = jnp.asarray(basis), jnp.asarray(pair), jnp.asarray(select, dtype=BF16)
    state = tangent.reshape(2 * ELEMS, NODES)
    swirl = base_swirl.reshape(ELEMS, NODES)
    slots = face_slot.T
    ids = corners.T
    field = jax.ShapeDtypeStruct((2 * ELEMS, NODES), F32)
    square = jax.ShapeDtypeStruct((NODES, NODES), BF16)
    faces = pltpu.VMEM((FACES * ELEMS, 2 * HALO), BF16)

    s1, msg, p, bm, bh, bl = call(
        first_kernel,
        [
            field,
            jax.ShapeDtypeStruct((8, MSG1, 128), F32),
            jax.ShapeDtypeStruct((FACES * ELEMS, FACES * ELEMS), BF16),
            jax.ShapeDtypeStruct((128, 8 * ELEMS), BF16),
            square,
            square,
        ],
        [faces],
        [state, swirl, metric, stiffness, slots, ids, select, basis, pair],
        4_000_000_000,
    )
    got = lax.all_to_all(msg, "dom", 0, 0)
    s2, msg = call(
        second_kernel,
        [field, jax.ShapeDtypeStruct((8, MSG2, 128), F32)],
        [faces],
        [s1, got, p, bm, bh, bl, swirl, metric, slots, ids, select, basis, pair, coarse_inverse],
        4_000_000_000,
    )
    size = lax.axis_size("seg")
    ring = [(i, (i + 1) % size) for i in range(size)]
    s2 = lax.ppermute(s2, "seg", ring)
    got = lax.all_to_all(msg, "dom", 0, 0)
    (small,) = call(
        pack_kernel,
        [jax.ShapeDtypeStruct((8 + HALO, 128), F32)],
        [],
        [got, coarse_inverse],
        100_000_000,
    )
    small = lax.ppermute(small, "seg", ring)
    (out,) = call(
        last_kernel,
        [field],
        [],
        [state, s2, small, bm, slots, ids, select, basis, phase_angle],
        1_000_000_000,
        [VMEM] * 8 + [SMEM],
    )
    return out.reshape(1, 2, ELEMS, NODES)


def solution(mesh):
    return jax.shard_map(
        shards,
        mesh=mesh,
        in_specs=(
            P("seg", None, "dom", None),
            P("seg", "dom", None),
            P("dom", None),
            P(),
            P("dom", None),
            P("dom", None),
            P(),
            P(),
        ),
        out_specs=P("seg", None, "dom", None),
        check_vma=False,
    )
```

profile of v0, /device:TPU:200, one launch (start us, length us, event | category | flops | bytes accessed | tf_op | source)
XLA Modules:
  0.0 79.1 jit_solution(5920677986436504071)
XLA Ops:
  0.0 1.2 %copy-done = f32[1,2,256,512]{3,2,1,0:T(8,128)S(1)} copy-done((f32[1,2,256,512]{3,2,1,0:T(8,128)S(1)}, f32[1,2,256,512]{3,2,1,0:T(8,128)}, u32[]{:S(2)}) %copy-start) | copy-done | bytes 1048600
  1.2 1.0 %copy-done.3 = bf16[512,384]{1,0:T(8,128)(2,1)S(1)} copy-done((bf16[512,384]{1,0:T(8,128)(2,1)S(1)}, bf16[512,384]{1,0:T(8,128)(2,1)}, u32[]{:S(2)}) %copy-start.3) | copy-done | bytes 393240
  2.2 0.7 copy-done.5
  2.9 0.7 copy-done.7
  3.6 0.7 copy-done.9
  4.3 1.0 %copy-done.11 = f32[1,256,512]{2,1,0:T(8,128)S(1)} copy-done((f32[1,256,512]{2,1,0:T(8,128)S(1)}, f32[1,256,512]{2,1,0:T(8,128)}, u32[]{:S(2)}) %copy-start.11) | copy-done | bytes 524312
  5.4 1.0 %copy-done.13 = f32[256,512]{1,0:T(8,128)S(1)} copy-done((f32[256,512]{1,0:T(8,128)S(1)}, f32[256,512]{1,0:T(8,128)}, u32[]{:S(2)}) %copy-start.13) | copy-done | bytes 524312
  6.4 0.7 copy-done.15
  7.1 0.7 copy-done.16
  7.8 0.0 copy-start.10
  7.8 0.0 copy-start.12
  7.8 0.0 copy-start.14
  7.8 0.0 copy-start.17
  7.8 5.5 %shard_map.109 = (f32[512,512]{1,0:T(8,128)S(1)}, f32[8,88,128]{2,1,0:T(8,128)S(1)}, bf16[1536,1536]{1,0:T(8,128)(2,1)S(1)}, bf16[128,2048]{1,0:T(8,128)(2,1)S(1...) custom-call(f32[512,512]{1,0:T(8,128)S(1)} %bitcast.5, f32[256,512]{1,0:T(8,128)S(1)} %bitcast.13, ...), custom_call_target="tpu_custom_call" | custom-call | flops 4000000000 | bytes 10225920 | tf_op jit(solution)/shard_map/pallas_call | solution.py:388
  13.3 24.7 %all_to_all.10.got_ref = f32[8,88,128]{2,1,0:T(8,128)S(1)} all-to-all(f32[8,88,128]{2,1,0:T(8,128)S(1)} %get-tuple-element.14), channel_id=1, replica_groups=mesh['seg'=64,'dom'=8] {'dom'}, dimensions={0} | all-to-all | bytes 720896 | tf_op jit(solution)/shard_map/all_to_all | solution.py:424
  38.0 0.0 copy-done.2
  38.0 0.0 copy-done.6
  38.0 0.0 copy-done.8
  38.0 0.0 copy-done.10
  38.0 0.0 copy-done.12
  38.0 0.0 copy-done.14
  38.1 0.0 copy-done.17
  38.1 0.0 copy-start.1
  38.1 6.6 %shard_map.110 = (f32[512,512]{1,0:T(8,128)S(1)}, f32[8,72,128]{2,1,0:T(8,128)S(1)}) custom-call(f32[512,512]{1,0:T(8,128)S(1)} %get-tuple-element.13.s1_ref, f32[8,88,128]{2,1,0:T(8,128)S(1)} %all_to_all.10.got_ref, bf16[1536,1536]{1,0:T(8,128)(2,1)S(1)} %get-tuple-element.15.p_ref, bf16[128,2048]{1,0:T(8,128)(2,1)S(1)} %get-tuple-element.16.bm_ref, ...), custom_call_target="tpu_custom_call" | custom-call | flops 4000000000 | bytes 11569152 | tf_op jit(solution)/shard_map/pallas_call | solution.py:388
  44.6 1.9 %collective-permute-start = (f32[512,512]{1,0:T(8,128)S(1)}, f32[512,512]{1,0:T(8,128)S(1)}, u32[]{:S(2)}, u32[]{:S(2)}) collective-permute-start(f32[512,512]{1,0:T(8,128)S(1)} %get-tuple-element.19), channel_id=1, source_target_pairs={{0,8},{8,16},{16,24},{24,32},{32,40},{40,48},{48,56},{56,64},{64,7... | collective-permute-start | bytes 3145736 | tf_op jit(solution)/shard_map/ppermute | solution.py:434
  46.6 23.8 %all_to_all.11.got_ref = f32[8,72,128]{2,1,0:T(8,128)S(1)} all-to-all(f32[8,72,128]{2,1,0:T(8,128)S(1)} %get-tuple-element.20), channel_id=1, replica_groups=mesh['seg'=64,'dom'=8] {'dom'}, dimensions={0} | all-to-all | bytes 589824 | tf_op jit(solution)/shard_map/all_to_all | solution.py:435
  70.4 0.4 shard_map.111
  70.8 2.0 %collective-permute-start.1 = (f32[136,128]{1,0:T(8,128)S(1)}, f32[136,128]{1,0:T(8,128)S(1)}, u32[]{:S(2)}, u32[]{:S(2)}) collective-permute-start(f32[136,128]{1,0:T(8,128)S(1)} %shard_map.111), channel_id=1, source_target_pairs={{0,8},{8,16},{16,24},{24,32},{32,40},{40,48},{48,56},{56,64},{64,7... | collective-permute-start | bytes 208904 | tf_op jit(solution)/shard_map/ppermute | solution.py:443
  73.5 3.0 %collective-permute-done.1.small_ref = f32[136,128]{1,0:T(8,128)S(1)} collective-permute-done((f32[136,128]{1,0:T(8,128)S(1)}, f32[136,128]{1,0:T(8,128)S(1)}, u32[]{:S(2)}, u32[]{:S(2)}) %collective-permute-start.1) | collective-permute-done | bytes 69664 | tf_op jit(solution)/shard_map/ppermute | solution.py:443
  76.4 0.0 collective-permute-done.s2_ref
  76.4 0.0 copy-done.1
  76.4 2.7 %shard_map.112 = f32[512,512]{1,0:T(8,128)} custom-call(f32[512,512]{1,0:T(8,128)S(1)} %bitcast.6, f32[512,512]{1,0:T(8,128)S(1)} %collective-permute-done.s2_ref, f32[136,128]{1,0:T(8,128)S(1)} %collective-permute-done.1.small_ref, bf16[128,2048]{1,0:T(8,128)(2,1)S(1)} %get-tuple-element.16.bm_ref, s32[6,256]{1,0:T(8,128)S(1)} %bitcast.9, ...), custom_call_target="tpu_custom_call" | custom-call | flops 1000000000 | bytes 4163588 | tf_op jit(solution)/shard_map/pallas_call | solution.py:388
  (14 shorter events, 0.0 us)
Async XLA Ops:
  0.0 1.2 %copy-start = (f32[1,2,256,512]{3,2,1,0:T(8,128)S(1)}, f32[1,2,256,512]{3,2,1,0:T(8,128)}, u32[]{:S(2)}) copy-start(f32[1,2,256,512]{3,2,1,0:T(8,128)} %param.11) | copy-start | bytes 3145732
  1.2 1.0 %copy-start.3 = (bf16[512,384]{1,0:T(8,128)(2,1)S(1)}, bf16[512,384]{1,0:T(8,128)(2,1)}, u32[]{:S(2)}) copy-start(bf16[512,384]{1,0:T(8,128)(2,1)} %constant.8.clone.sel_ref) | copy-start | bytes 1179652
  2.2 0.7 copy-start.5
  2.9 0.7 copy-start.7
  3.6 0.7 copy-start.9
  4.3 1.0 %copy-start.11 = (f32[1,256,512]{2,1,0:T(8,128)S(1)}, f32[1,256,512]{2,1,0:T(8,128)}, u32[]{:S(2)}) copy-start(f32[1,256,512]{2,1,0:T(8,128)} %param.12) | copy-start | bytes 1572868
  5.4 1.0 %copy-start.13 = (f32[256,512]{1,0:T(8,128)S(1)}, f32[256,512]{1,0:T(8,128)}, u32[]{:S(2)}) copy-start(f32[256,512]{1,0:T(8,128)} %met_ref.3) | copy-start | bytes 1572868
  6.4 0.7 copy-start.15
  7.1 0.7 copy-start.16
  7.8 30.2 %copy-start.2 = (f32[512,512]{1,0:T(8,128)S(1)}, f32[512,512]{1,0:T(8,128)}, u32[]{:S(2)}) copy-start(f32[512,512]{1,0:T(8,128)} %inv_ref.3) | copy-start | bytes 3145732
  7.8 30.2 %copy-start.4 = (bf16[512,384]{1,0:T(8,128)(2,1)S(1)}, bf16[512,384]{1,0:T(8,128)(2,1)}, u32[]{:S(2)}) copy-start(bf16[512,384]{1,0:T(8,128)(2,1)} %constant.8.clone.sel_ref) | copy-start | bytes 1179652
  7.8 30.2 %copy-start.6 = (f32[8,512]{1,0:T(8,128)S(1)}, f32[8,512]{1,0:T(8,128)}, u32[]{:S(2)}) copy-start(f32[8,512]{1,0:T(8,128)} %constant.6.clone.bas_ref) | copy-start | bytes 49156
  7.8 30.2 %copy-start.8 = (s32[256,6]{0,1:T(8,128)S(1)}, s32[256,6]{0,1:T(8,128)}, u32[]{:S(2)}) copy-start(s32[256,6]{0,1:T(8,128)} %param.15) | copy-start | bytes 18436
  7.8 30.2 %copy-start.10 = (s32[256,8]{0,1:T(8,128)S(1)}, s32[256,8]{0,1:T(8,128)}, u32[]{:S(2)}) copy-start(s32[256,8]{0,1:T(8,128)} %param.16) | copy-start | bytes 24580
  7.8 30.2 %copy-start.12 = (f32[1,256,512]{2,1,0:T(8,128)S(1)}, f32[1,256,512]{2,1,0:T(8,128)}, u32[]{:S(2)}) copy-start(f32[1,256,512]{2,1,0:T(8,128)} %param.12) | copy-start | bytes 1572868
  7.8 30.2 %copy-start.14 = (f32[256,512]{1,0:T(8,128)S(1)}, f32[256,512]{1,0:T(8,128)}, u32[]{:S(2)}) copy-start(f32[256,512]{1,0:T(8,128)} %met_ref.3) | copy-start | bytes 1572868
  7.8 30.2 %copy-start.17 = (f32[8,128]{1,0:T(8,128)S(1)}, f32[8,128]{1,0:T(8,128)}, u32[]{:S(2)}) copy-start(f32[8,128]{1,0:T(8,128)} %constant.7.clone.pair_ref) | copy-start | bytes 12292
  38.1 38.4 %copy-start.1 = (f32[1,2,256,512]{3,2,1,0:T(8,128)S(1)}, f32[1,2,256,512]{3,2,1,0:T(8,128)}, u32[]{:S(2)}) copy-start(f32[1,2,256,512]{3,2,1,0:T(8,128)} %param.11) | copy-start | bytes 3145732
  44.6 31.8 %collective-permute-start = (f32[512,512]{1,0:T(8,128)S(1)}, f32[512,512]{1,0:T(8,128)S(1)}, u32[]{:S(2)}, u32[]{:S(2)}) collective-permute-start(f32[512,512]{1,0:T(8,128)S(1)} %get-tuple-element.19), channel_id=1, source_target_pairs={{0,8},{8,16},{16,24},{24,32},{32,40},{40,48},{48,56},{56,64},{64,7... | collective-permute-start | bytes 3145736 | tf_op jit(solution)/shard_map/ppermute | solution.py:434
  70.8 5.6 %collective-permute-start.1 = (f32[136,128]{1,0:T(8,128)S(1)}, f32[136,128]{1,0:T(8,128)S(1)}, u32[]{:S(2)}, u32[]{:S(2)}) collective-permute-start(f32[136,128]{1,0:T(8,128)S(1)} %shard_map.111), channel_id=1, source_target_pairs={{0,8},{8,16},{16,24},{24,32},{32,40},{40,48},{48,56},{56,64},{64,7... | collective-permute-start | bytes 208904 | tf_op jit(solution)/shard_map/ppermute | solution.py:443
where the time goes:
time: 79.7 us; the launch traced here: 79.1 us
  blocking collectives  48.5 us (61%)
  Pallas kernels  15.1 us (19%)
  local copies, waits for them, and re-layouts  7.82 us (10%)
  starting transfers between devices  3.94 us (5%)
  waiting for transfers between devices  2.97 us (4%)
    all_to_all x2, blocking collectives, shards(): got = lax.all_to_all(msg, 'dom', 0, 0)  48.5 us
    pallas_call x4, Pallas kernels, call(): pl.pallas_call(body, out_shape=outs, in_specs=specs or [VMEM] * len(ins),...  15.1 us
    unnamed x36, local copies, waits for them, and re-layouts  7.82 us
    ppermute x1, waiting for transfers between devices, shards(): small = lax.ppermute(small, 'seg', ring)  2.97 us
    ppermute x1, starting transfers between devices, shards(): small = lax.ppermute(small, 'seg', ring)  2.01 us
    ppermute x1, starting transfers between devices, shards(): s2 = lax.ppermute(s2, 'seg', ring)  1.93 us
  transfers between devices with their start and end apart: 2, of which 1 were waited for; matrix products, arithmetic and copies ran while one was open for 0% of the time, Pallas kernels for 0%

commit v1 on v0

--- a/solution.py
+++ b/solution.py
@@ -41,7 +41,7 @@
     pair[:4, :PLANE] = flat
     pair[4:, PLANE:] = flat
     node = np.arange(NODES).reshape(NP, NP, NP)
-    faces = [node[0], node[-1], node[:, 0], node[:, -1], node[:, :, 0], node[:, :, -1]]
+    faces = [node[:, 0], node[:, -1], node[:, :, 0], node[:, :, -1]]
     chosen = np.concatenate([f.reshape(-1) for f in faces])
     select = (np.arange(NODES)[:, None] == chosen[None, :]).astype(np.float32)
     return basis.astype(np.float32), pair.astype(np.float32), select
@@ -95,6 +95,11 @@
 
 def row_of(parts):
     return jnp.concatenate([parts[k : k + 1, :] for k in range(parts.shape[0])], axis=1)
+
+
+def stiff_of(state, bh, bl):
+    high, low = split(state)
+    return dot(high, bh) + dot(low, bh) + dot(high, bl)
 
 
 def stiff_matrix(sti):
@@ -118,26 +123,43 @@
     return total
 
 
-def advance(state, bh, bl, metric, swirl):
-    high, low = split(state)
-    stiff = dot(high, bh) + dot(low, bh) + dot(high, bl)
+def advance(state, stiff, metric, swirl):
     re, im = state[:ELEMS], state[ELEMS:]
     new_re = re - metric * stiff[:ELEMS] - swirl * im
     new_im = im - metric * stiff[ELEMS:] + swirl * re
     return jnp.concatenate([new_re, new_im], axis=0)
 
 
-def face_block(fh, fl, f):
-    lanes = slice(f * PLANE, (f + 1) * PLANE)
-    return jnp.concatenate(
-        [fh[:ELEMS, lanes], fh[ELEMS:, lanes], fl[:ELEMS, lanes], fl[ELEMS:, lanes]], axis=1
-    ).astype(BF16)
-
-
-def to_elements(blocks):
-    re = jnp.concatenate([b[:, :PLANE] for b in blocks], axis=1)
-    im = jnp.concatenate([b[:, PLANE:] for b in blocks], axis=1)
-    return jnp.concatenate([re, im], axis=0)
+def face_blocks(advanced, select):
+    ah, al = split(advanced)
+    fh, fl = dot(ah, select), dot(al, select)
+    high, low = ah.astype(F32), al.astype(F32)
+    ends = (slice(0, PLANE), slice(NODES - PLANE, NODES))
+    pairs = [(high[:, lanes], low[:, lanes]) for lanes in ends]
+    for f in range(4):
+        lanes = slice(f * PLANE, (f + 1) * PLANE)
+        pairs.append((fh[:, lanes], fl[:, lanes]))
+    blocks = [
+        jnp.concatenate([h[:ELEMS], h[ELEMS:], l[:ELEMS], l[ELEMS:]], axis=1).astype(BF16) for h, l in pairs
+    ]
+    return blocks, ah, al
+
+
+def scattered(blocks, select):
+    def element_rows(faces, offset):
+        re = jnp.concatenate([b[:, offset : offset + PLANE] for b in faces], axis=1)
+        im = jnp.concatenate([b[:, offset + PLANE : offset + 2 * PLANE] for b in faces], axis=1)
+        return jnp.concatenate([re, im], axis=0)
+
+    high = element_rows(blocks[2:], 0).astype(BF16)
+    low = element_rows(blocks[2:], HALO).astype(BF16)
+    inner = dot_nt(high, select) + dot_nt(low, select)
+    ends = []
+    for block in blocks[:2]:
+        both = block[:, :HALO] + block[:, HALO:]
+        ends.append(jnp.concatenate([both[:, :PLANE], both[:, PLANE:]], axis=0))
+    gap = jnp.zeros((2 * ELEMS, NODES - 2 * PLANE), F32)
+    return inner + jnp.concatenate([ends[0], gap, ends[1]], axis=1)
 
 
 def multiplicity():
@@ -160,24 +182,25 @@
     return jnp.where(iota((8, 1), 0) < 4, re, im)
 
 
-def coarse_of(settled, basis, cvh_row, bm):
-    sh, sl = split(settled)
-    scaled = basis * F32(1.0 / NODES)
-    two = stacked(scaled)
-    first = dot_nt(two, sh)
-    second = dot_nt(two, sl)
-    r = first[:8] + first[8:] + second[:8]
-    re = row_of(r[:, :ELEMS])
-    im = row_of(r[:, ELEMS:])
-    return deposit(eight(re, im), cvh_row, bm)
-
-
-def face_restricted(yh, yl, pair):
-    scaled = pair * F32(0.5 / NODES)
-    two = stacked(scaled)
-    first = dot_nt(two, yh.astype(BF16))
-    second = dot_nt(two, yl.astype(BF16))
+def two_products(table, high, low):
+    first = dot_nt(stacked(table), high)
+    second = dot_nt(stacked(table), low)
     return first[:8] + first[8:] + second[:8]
+
+
+def coarse_of(ah, al, partner, basis, pair, cvh, bm):
+    own = two_products(basis * ((F32(1.0) - F32(0.5) * multiplicity()) * F32(1.0 / NODES)), ah, al)
+    lifted = two_products(pair * F32(0.5 / NODES), partner[:, :HALO], partner[:, HALO:])
+    values = []
+    for k in range(8):
+        total = eight(own[k : k + 1, :ELEMS], own[k : k + 1, ELEMS:])
+        for f in range(FACES):
+            if k in FACE_CORNERS[f]:
+                r = FACE_CORNERS[f].index(k)
+                lanes = slice(f * ELEMS, (f + 1) * ELEMS)
+                total = total + eight(lifted[r : r + 1, lanes], lifted[4 + r : 5 + r, lanes])
+        values.append(total)
+    return deposit(jnp.concatenate(values, axis=1), row_of(cvh), bm)
 
 
 def solve(coarse, kh, kl):
@@ -193,7 +216,7 @@
     )
 
 
-def correction(solved, basis, cvh_row, bm):
+def corner_values(solved, cvh_row, bm):
     both = dot(stacked(solved), bm)
     spread = both[:8] + both[8:]
     vh = (iota((8, 1), 0) & 3).astype(F32)
@@ -204,10 +227,12 @@
         lines.append(jnp.concatenate([line[:, ELEMS * k : ELEMS * (k + 1)] for k in range(8)], axis=0))
     by_corner = jnp.concatenate(lines, axis=1)
     high = by_corner.astype(BF16).astype(F32)
-    left = jnp.concatenate([high, by_corner - high, high, jnp.zeros((8, NODES), F32)], axis=0)
-    bas_high = basis.astype(BF16).astype(F32)
-    right = jnp.concatenate([bas_high, bas_high, basis - bas_high, jnp.zeros((8, NODES), F32)], axis=0)
-    return dot_tn(left.astype(BF16), right.astype(BF16))
+    return jnp.concatenate([high, by_corner - high, high, jnp.zeros((8, NODES), F32)], axis=0).astype(BF16)
+
+
+def tripled(table):
+    high = table.astype(BF16).astype(F32)
+    return jnp.concatenate([high, high, table - high, jnp.zeros_like(high)], axis=0).astype(BF16)
 
 
 def shared_target_column():
@@ -220,34 +245,25 @@
     return jnp.where(s < SHARED, s, s + (INNER_TOP - SHARED)).astype(F32)
 
 
-def halo_part(columns, arrived, select):
+def halo_part(placed, arrived, select):
     high, low = split(arrived)
     both = jnp.concatenate([high.astype(F32), low.astype(F32)], axis=1).astype(BF16)
-    target = shared_target_row()
-    blocks_h, blocks_l = [], []
+    got = dot(placed, both)
+    return scattered([got[f * ELEMS : (f + 1) * ELEMS] for f in range(FACES)], select)
+
+
+def settle(advanced, partner, select):
+    blocks = [partner[f * ELEMS : (f + 1) * ELEMS].astype(F32) for f in range(FACES)]
+    kept = advanced * (F32(1.0) - F32(0.5) * multiplicity())
+    return kept + F32(0.5) * scattered(blocks, select)
+
+
+def pair_up(blocks, p_ref, q_ref, g_ref):
     for f in range(FACES):
-        got = dot(hot(columns[f] == target), both)
-        blocks_h.append(got[:, :HALO])
-        blocks_l.append(got[:, HALO:])
-    return dot_nt(to_elements(blocks_h).astype(BF16), select) + dot_nt(
-        to_elements(blocks_l).astype(BF16), select
-    )
-
-
-def local_settle(advanced, select, pairing, q_ref, out_ref):
-    ah, al = split(advanced)
-    fh = dot(ah, select)
-    fl = dot(al, select)
+        q_ref[f * ELEMS : (f + 1) * ELEMS, :] = blocks[f]
     for f in range(FACES):
-        q_ref[f * ELEMS : (f + 1) * ELEMS, :] = face_block(fh, fl, f)
-    blocks = []
-    for f in range(FACES):
-        got = dot(pairing(f), q_ref[...])
-        blocks.append(got[:, :HALO] + got[:, HALO:])
-    gathered = to_elements(blocks)
-    gh, gl = split(gathered)
-    lift = dot_nt(gh, select) + dot_nt(gl, select)
-    out_ref[...] = advanced * (F32(1.0) - multiplicity()) + F32(0.5) * lift
+        rows = slice(f * ELEMS, (f + 1) * ELEMS)
+        g_ref[rows, :] = dot(p_ref[rows, :], q_ref[...]).astype(BF16)
 
 
 def send_rows(msg_ref, me, head, rows):
@@ -260,32 +276,47 @@
 
 
 def first_kernel(
-    tan_ref, swl_ref, met_ref, sti_ref, fs_ref, cor_ref, sel_ref, bas_ref, pair_ref,
-    out_ref, msg_ref, p_ref, bm_ref, bh_ref, bl_ref, q_ref,
+    tan_hbm, swl_hbm, met_hbm, sti_hbm, fs_hbm, cor_hbm, sel_hbm, bas_hbm, pair_hbm, inv_hbm,
+    out_ref, msg_ref, p_ref, bm_ref, bh_ref, bl_ref, kh_ref, kl_ref, pl_ref, lb_ref,
+    q_ref, g_ref, tan_ref, swl_ref, met_ref, sti_ref, fs_ref, cor_ref, sel_ref, bas_ref, pair_ref, inv_ref, sems,
 ):
     me = lax.axis_index("dom")
+    moves = [
+        pltpu.make_async_copy(src, dst, sems.at[i])
+        for i, (src, dst) in enumerate(
+            (
+                (sti_hbm, sti_ref),
+                (fs_hbm, fs_ref),
+                (cor_hbm, cor_ref),
+                (tan_hbm, tan_ref),
+                (met_hbm, met_ref),
+                (swl_hbm, swl_ref),
+                (sel_hbm, sel_ref),
+                (bas_hbm, bas_ref),
+                (pair_hbm, pair_ref),
+                (inv_hbm, inv_ref),
+            )
+        )
+    ]
+    for move in moves:
+        move.start()
+    for move in moves[:3]:
+        move.wait()
     bh, bl = split(stiff_matrix(sti_ref[...]))
     bh_ref[...] = bh
     bl_ref[...] = bl
     rows = slot_rows(fs_ref)
-    row = jnp.concatenate(rows, axis=1)
     columns = slot_columns(fs_ref)
+    other = iota((ELEMS, 1), 0) != iota((1, ELEMS), 1)
     for f in range(FACES):
-        p_ref[f * ELEMS : (f + 1) * ELEMS, :] = hot(columns[f] == row)
+        for g in range(FACES):
+            same = columns[f] == rows[g]
+            if f == g:
+                same = same & other
+            p_ref[f * ELEMS : (f + 1) * ELEMS, g * ELEMS : (g + 1) * ELEMS] = hot(same)
     cvh, cvl = corner_parts(cor_ref)
-    cvh_row = row_of(cvh)
     bm_ref[...] = hot(row_of(cvl) == iota((128, 1), 0).astype(F32))
-    basis = bas_ref[...]
-
-    advanced = advance(tan_ref[...], bh_ref[...], bl_ref[...], met_ref[...], swl_ref[...])
-    local_settle(
-        advanced, sel_ref[...], lambda f: p_ref[f * ELEMS : (f + 1) * ELEMS, :], q_ref, out_ref
-    )
-    coarse = coarse_of(out_ref[...], basis, cvh_row, bm_ref[...])
-    shared = hot(shared_target_column() == row)
-    y = dot(shared, q_ref[...])
-    yh, yl = y[:, :HALO], y[:, HALO:]
-    rf = face_restricted(yh, yl, pair_ref[...])
+    shared = hot(shared_target_column() == jnp.concatenate(rows, axis=1))
     face_ids = jnp.concatenate(
         [
             jnp.concatenate(
@@ -298,24 +329,46 @@
         axis=0,
     ).astype(BF16)
     ids = dot_nt(face_ids, shared)[:8]
+    target = shared_target_row()
+    for f in range(FACES):
+        pl_ref[f * ELEMS : (f + 1) * ELEMS, :] = hot(columns[f] == target)
+    for move in moves[3:]:
+        move.wait()
+    basis = bas_ref[...]
+    stiff = stiff_of(jnp.concatenate([basis, basis], axis=0), bh_ref[...], bl_ref[...])
+    lb_ref[:, :NODES] = tripled(basis)
+    lb_ref[:, NODES:] = tripled(stiff[:8])
+    kh, kl = split(inv_ref[...])
+    kh_ref[...] = kh
+    kl_ref[...] = kl
+
+    state = tan_ref[...]
+    advanced = advance(state, stiff_of(state, bh_ref[...], bl_ref[...]), met_ref[...], swl_ref[...])
+    blocks, ah, al = face_blocks(advanced, sel_ref[...])
+    pair_up(blocks, p_ref, q_ref, g_ref)
+    out_ref[...] = settle(advanced, g_ref[...], sel_ref[...])
+    coarse = coarse_of(ah, al, g_ref[...], bas_ref[...], pair_ref[...], cvh, bm_ref[...])
+    y = dot(shared, q_ref[...])
+    yh, yl = y[:, :HALO], y[:, HALO:]
+    rf = two_products(pair_ref[...] * F32(0.5 / NODES), yh.astype(BF16), yl.astype(BF16))
     send_rows(msg_ref, me, jnp.concatenate([coarse, rf, ids], axis=0), yh + yl)
 
 
 def second_kernel(
-    s1_ref, got_ref, p_ref, bm_ref, bh_ref, bl_ref, swl_ref, met_ref, fs_ref, cor_ref, sel_ref, bas_ref,
-    pair_ref, inv_ref,
-    out_ref, msg_ref, q_ref,
+    s1_ref, got_ref, p_ref, bm_ref, bh_ref, bl_ref, kh_ref, kl_ref, pl_ref, lb_ref, swl_ref, met_ref, fs_ref, cor_ref,
+    sel_ref, bas_ref, pair_ref,
+    out_ref, msg_ref, q_ref, g_ref,
 ):
     me = lax.axis_index("dom")
     before, after = lax.rem(me + 7, 8), lax.rem(me + 1, 8)
-    kh, kl = split(inv_ref[...])
-    basis = bas_ref[...]
     select = sel_ref[...]
-    columns = slot_columns(fs_ref)
-    row = jnp.concatenate(slot_rows(fs_ref), axis=1)
     cvh, _ = corner_parts(cor_ref)
     cvh_row = row_of(cvh)
     which = iota((128, 1), 0).astype(F32)
+
+    arrived = jnp.concatenate([got_ref[before, 24:MSG1, :], got_ref[after, 24:MSG1, :]], axis=0)
+    partly = s1_ref[...] + F32(0.5) * halo_part(pl_ref[...], arrived, select)
+    stiff = stiff_of(partly, bh_ref[...], bl_ref[...])
 
     coarse = got_ref[0, 0:8, :]
     for j in range(1, 8):
@@ -330,21 +383,17 @@
         coarse = coarse + deposit(
             eight(rf[r : r + 1, :], rf[4 + r : 5 + r, :]), partner[r : r + 1, :], low_hot
         )
-    solved = solve(coarse, kh, kl)
-
-    arrived = jnp.concatenate([got_ref[before, 24:MSG1, :], got_ref[after, 24:MSG1, :]], axis=0)
-    current = (
-        s1_ref[...]
-        + F32(0.5) * halo_part(columns, arrived, select)
-        - correction(solved, basis, cvh_row, bm_ref[...])
-    )
-    advanced = advance(current, bh_ref[...], bl_ref[...], met_ref[...], swl_ref[...])
-    local_settle(advanced, select, lambda f: p_ref[f * ELEMS : (f + 1) * ELEMS, :], q_ref, out_ref)
-    coarse = coarse_of(out_ref[...], basis, cvh_row, bm_ref[...])
-    shared = hot(shared_target_column() == row)
+    solved = solve(coarse, kh_ref[...], kl_ref[...])
+    both = dot_tn(corner_values(solved, cvh_row, bm_ref[...]), lb_ref[...])
+    advanced = advance(partly - both[:, :NODES], stiff - both[:, NODES:], met_ref[...], swl_ref[...])
+    blocks, ah, al = face_blocks(advanced, select)
+    pair_up(blocks, p_ref, q_ref, g_ref)
+    out_ref[...] = settle(advanced, g_ref[...], select)
+    coarse = coarse_of(ah, al, g_ref[...], bas_ref[...], pair_ref[...], cvh, bm_ref[...])
+    shared = hot(shared_target_column() == jnp.concatenate(slot_rows(fs_ref), axis=1))
     y = dot(shared, q_ref[...])
     yh, yl = y[:, :HALO], y[:, HALO:]
-    rf = face_restricted(yh, yl, pair_ref[...])
+    rf = two_products(pair_ref[...] * F32(0.5 / NODES), yh.astype(BF16), yl.astype(BF16))
     mine = jnp.concatenate([got_ref[before, 16:24, SHARED:], got_ref[after, 16:24, :SHARED]], axis=1)
     for r in range(4):
         low_hot = hot(mine[4 + r : 5 + r, :] == which)
@@ -352,23 +401,23 @@
     send_rows(msg_ref, me, coarse, yh + yl)
 
 
-def pack_kernel(got_ref, inv_ref, out_ref):
+def pack_kernel(got_ref, kh_ref, kl_ref, out_ref):
     me = lax.axis_index("dom")
-    kh, kl = split(inv_ref[...])
     coarse = got_ref[0, 0:8, :]
     for j in range(1, 8):
         coarse = coarse + got_ref[j, 0:8, :]
-    out_ref[0:8, :] = solve(coarse, kh, kl)
+    out_ref[0:8, :] = solve(coarse, kh_ref[...], kl_ref[...])
     out_ref[8 : 8 + SHARED, :] = got_ref[lax.rem(me + 7, 8), 8:MSG2, :]
     out_ref[8 + SHARED :, :] = got_ref[lax.rem(me + 1, 8), 8:MSG2, :]
 
 
-def last_kernel(tan_ref, s2_ref, small_ref, bm_ref, fs_ref, cor_ref, sel_ref, bas_ref, ang_ref, out_ref):
+def last_kernel(tan_ref, s2_ref, small_ref, bm_ref, pl_ref, lb_ref, cor_ref, sel_ref, ang_ref, out_ref):
     cvh, _ = corner_parts(cor_ref)
+    corners = corner_values(small_ref[0:8, :], row_of(cvh), bm_ref[...])
     state = (
         s2_ref[...]
-        + F32(0.5) * halo_part(slot_columns(fs_ref), small_ref[8:, :], sel_ref[...])
-        - correction(small_ref[0:8, :], bas_ref[...], row_of(cvh), bm_ref[...])
+        + F32(0.5) * halo_part(pl_ref[...], small_ref[8:, :], sel_ref[...])
+        - dot_tn(corners, lb_ref[:, :NODES])
     )
     angle = jnp.where(lax.axis_index("seg") == 0, ang_ref[0], F32(0.0))
     angles = jnp.full((1, NODES), angle, F32)
@@ -380,9 +429,10 @@
 
 VMEM = pl.BlockSpec(memory_space=pltpu.VMEM)
 SMEM = pl.BlockSpec(memory_space=pltpu.SMEM)
-
-
-def call(body, outs, scratch, ins, flops, specs=None, limit=40):
+HBM = pl.BlockSpec(memory_space=pltpu.HBM)
+
+
+def call(body, outs, scratch, ins, flops, specs=None, limit=28):
     size = sum(int(np.prod(o.shape)) * o.dtype.itemsize for o in outs)
     size += sum(int(np.prod(a.shape)) * a.dtype.itemsize for a in ins)
     return pl.pallas_call(
@@ -396,6 +446,10 @@
     )(*ins)
 
 
+def like(*shape, dtype=F32):
+    return jax.ShapeDtypeStruct(shape, dtype)
+
+
 def shards(tangent, base_swirl, metric, stiffness, face_slot, corners, coarse_inverse, phase_angle):
     basis, pair, select = tables()
     basis, pair, select = jnp.asarray(basis), jnp.asarray(pair), jnp.asarray(select, dtype=BF16)
@@ -403,49 +457,50 @@
     swirl = base_swirl.reshape(ELEMS, NODES)
     slots = face_slot.T
     ids = corners.T
-    field = jax.ShapeDtypeStruct((2 * ELEMS, NODES), F32)
-    square = jax.ShapeDtypeStruct((NODES, NODES), BF16)
-    faces = pltpu.VMEM((FACES * ELEMS, 2 * HALO), BF16)
-
-    s1, msg, p, bm, bh, bl = call(
+    field = like(2 * ELEMS, NODES)
+    square = like(NODES, NODES, dtype=BF16)
+    count = FACES * ELEMS
+    faces = pltpu.VMEM((count, 2 * HALO), BF16)
+
+    ins = [state, swirl, metric, stiffness, slots, ids, select, basis, pair, coarse_inverse]
+    s1, msg, p, bm, bh, bl, kh, kl, placed, lb = call(
         first_kernel,
         [
             field,
-            jax.ShapeDtypeStruct((8, MSG1, 128), F32),
-            jax.ShapeDtypeStruct((FACES * ELEMS, FACES * ELEMS), BF16),
-            jax.ShapeDtypeStruct((128, 8 * ELEMS), BF16),
+            like(8, MSG1, 128),
+            like(count, count, dtype=BF16),
+            like(128, 8 * ELEMS, dtype=BF16),
             square,
             square,
+            square,
+            square,
+            like(count, HALO, dtype=BF16),
+            like(32, 2 * NODES, dtype=BF16),
         ],
-        [faces],
-        [state, swirl, metric, stiffness, slots, ids, select, basis, pair],
+        [faces, faces] + [pltpu.VMEM(a.shape, a.dtype) for a in ins] + [pltpu.SemaphoreType.DMA((len(ins),))],
+        [pltpu.with_memory_space_constraint(a, pltpu.HBM) for a in ins],
         4_000_000_000,
+        [HBM] * len(ins),
     )
     got = lax.all_to_all(msg, "dom", 0, 0)
     s2, msg = call(
         second_kernel,
-        [field, jax.ShapeDtypeStruct((8, MSG2, 128), F32)],
-        [faces],
-        [s1, got, p, bm, bh, bl, swirl, metric, slots, ids, select, basis, pair, coarse_inverse],
+        [field, like(8, MSG2, 128)],
+        [faces, faces],
+        [s1, got, p, bm, bh, bl, kh, kl, placed, lb, swirl, metric, slots, ids, select, basis, pair],
         4_000_000_000,
     )
     size = lax.axis_size("seg")
     ring = [(i, (i + 1) % size) for i in range(size)]
+    got = lax.all_to_all(msg, "dom", 0, 0)
     s2 = lax.ppermute(s2, "seg", ring)
-    got = lax.all_to_all(msg, "dom", 0, 0)
-    (small,) = call(
-        pack_kernel,
-        [jax.ShapeDtypeStruct((8 + HALO, 128), F32)],
-        [],
-        [got, coarse_inverse],
-        100_000_000,
-    )
+    (small,) = call(pack_kernel, [like(8 + HALO, 128)], [], [got, kh, kl], 100_000_000)
     small = lax.ppermute(small, "seg", ring)
     (out,) = call(
         last_kernel,
         [field],
         [],
-        [state, s2, small, bm, slots, ids, select, basis, phase_angle],
+        [state, s2, small, bm, placed, lb, ids, select, phase_angle],
         1_000_000_000,
         [VMEM] * 8 + [SMEM],
     )

time: 79.7 us -> 73.3 us (0.920)
  local copies, waits for them, and re-layouts: 7.82 us -> 0.04 us
  Pallas kernels: 15.1 us -> 16.9 us
    unnamed x36 -> x16, local copies, waits for them, and re-layouts: 7.82 us -> 0.04 us
    pallas_call x4, Pallas kernels: 15.1 us -> 16.9 us  [call(): pl.pallas_call(body, out_shape=outs, in_specs=specs or [VMEM] * len(ins),...]
  transfers between devices with their start and end apart: 2 -> 2, of which waited for: 1 -> 1; matrix products, arithmetic and copies ran while one was open for 0% -> 0% of each run, Pallas kernels for 0% -> 1%
where the time goes in v1:
time: 73.3 us; the launch traced here: 73.1 us
  blocking collectives  48.5 us (66%)
  Pallas kernels  16.9 us (23%)
  starting transfers between devices  3.95 us (5%)
  waiting for transfers between devices  2.97 us (4%)
  between operations  0.75 us (1%)
    all_to_all x2, blocking collectives, shards(): got = lax.all_to_all(msg, 'dom', 0, 0)  48.5 us
    pallas_call x4, Pallas kernels, call(): pl.pallas_call(body, out_shape=outs, in_specs=specs or [VMEM] * len(ins),...  16.9 us
    ppermute x1, waiting for transfers between devices, shards(): small = lax.ppermute(small, 'seg', ring)  2.97 us
    ppermute x1, starting transfers between devices, shards(): small = lax.ppermute(small, 'seg', ring)  2.01 us
    ppermute x1, starting transfers between devices, shards(): s2 = lax.ppermute(s2, 'seg', ring)  1.93 us
  transfers between devices with their start and end apart: 2, of which 1 were waited for; matrix products, arithmetic and copies ran while one was open for 0% of the time, Pallas kernels for 1%

profile of v1, /device:TPU:200, one launch (start us, length us, event | category | flops | bytes accessed | tf_op | source)
XLA Modules:
  0.0 73.1 jit_solution(10446458052796041697)
XLA Ops:
  0.0 0.0 copy-start.1
  0.0 0.0 copy-start.2
  0.0 0.0 copy-start.3
  0.0 0.0 copy-start.4
  0.0 0.0 copy-start.5
  0.0 0.0 copy-start.6
  0.0 0.0 copy-start.7
  0.1 7.7 %shard_map.109 = (f32[512,512]{1,0:T(8,128)S(1)}, f32[8,88,128]{2,1,0:T(8,128)S(1)}, bf16[1536,1536]{1,0:T(8,128)(2,1)S(1)}, bf16[128,2048]{1,0:T(8,128)(2,1)S(1...) custom-call(f32[512,512]{1,0:T(8,128)} %bitcast.5, ...), custom_call_target="tpu_custom_call" | custom-call | flops 4000000000 | bytes 12650752 | tf_op jit(solution)/shard_map/pallas_call | solution.py:438
  7.7 24.7 %all_to_all.10.got_ref = f32[8,88,128]{2,1,0:T(8,128)S(1)} all-to-all(f32[8,88,128]{2,1,0:T(8,128)S(1)} %get-tuple-element.18), channel_id=1, replica_groups=mesh['seg'=64,'dom'=8] {'dom'}, dimensions={0} | all-to-all | bytes 720896 | tf_op jit(solution)/shard_map/all_to_all | solution.py:485
  32.4 0.0 copy-done.1
  32.4 0.0 copy-done.2
  32.4 0.0 copy-done.3
  32.4 0.0 copy-done.4
  32.4 0.0 copy-done.5
  32.4 0.0 copy-done.6
  32.4 0.0 copy-done.7
  32.5 0.0 copy-start
  32.5 6.6 %shard_map.110 = (f32[512,512]{1,0:T(8,128)S(1)}, f32[8,72,128]{2,1,0:T(8,128)S(1)}) custom-call(f32[512,512]{1,0:T(8,128)S(1)} %get-tuple-element.17.s1_ref, f32[8,88,128]{2,1,0:T(8,128)S(1)} %all_to_all.10.got_ref, bf16[1536,1536]{1,0:T(8,128)(2,1)S(1)} %get-tuple-element.19.p_ref, bf16[128,2048]{1,0:T(8,128)(2,1)S(1)} %get-tuple-element.20.bm_ref, ...), custom_call_target="tpu_custom_call" | custom-call | flops 4000000000 | bytes 11896832 | tf_op jit(solution)/shard_map/pallas_call | solution.py:438
  39.1 1.9 %collective-permute-start = (f32[512,512]{1,0:T(8,128)S(1)}, f32[512,512]{1,0:T(8,128)S(1)}, u32[]{:S(2)}, u32[]{:S(2)}) collective-permute-start(f32[512,512]{1,0:T(8,128)S(1)} %get-tuple-element.27), channel_id=1, source_target_pairs={{0,8},{8,16},{16,24},{24,32},{32,40},{40,48},{48,56},{56,64},{64,7... | collective-permute-start | bytes 3145736 | tf_op jit(solution)/shard_map/ppermute | solution.py:496
  41.0 23.8 %all_to_all.11.got_ref = f32[8,72,128]{2,1,0:T(8,128)S(1)} all-to-all(f32[8,72,128]{2,1,0:T(8,128)S(1)} %get-tuple-element.28), channel_id=1, replica_groups=mesh['seg'=64,'dom'=8] {'dom'}, dimensions={0} | all-to-all | bytes 589824 | tf_op jit(solution)/shard_map/all_to_all | solution.py:495
  64.9 0.4 shard_map.111
  65.2 2.0 %collective-permute-start.1 = (f32[136,128]{1,0:T(8,128)S(1)}, f32[136,128]{1,0:T(8,128)S(1)}, u32[]{:S(2)}, u32[]{:S(2)}) collective-permute-start(f32[136,128]{1,0:T(8,128)S(1)} %shard_map.111), channel_id=1, source_target_pairs={{0,8},{8,16},{16,24},{24,32},{32,40},{40,48},{48,56},{56,64},{64,7... | collective-permute-start | bytes 208904 | tf_op jit(solution)/shard_map/ppermute | solution.py:498
  67.9 3.0 %collective-permute-done.1.small_ref = f32[136,128]{1,0:T(8,128)S(1)} collective-permute-done((f32[136,128]{1,0:T(8,128)S(1)}, f32[136,128]{1,0:T(8,128)S(1)}, u32[]{:S(2)}, u32[]{:S(2)}) %collective-permute-start.1) | collective-permute-done | bytes 69664 | tf_op jit(solution)/shard_map/ppermute | solution.py:498
  70.9 0.0 collective-permute-done.s2_ref
  70.9 0.0 copy-done
  70.9 2.2 %shard_map.112 = f32[512,512]{1,0:T(8,128)} custom-call(f32[512,512]{1,0:T(8,128)S(1)} %bitcast.6, f32[512,512]{1,0:T(8,128)S(1)} %collective-permute-done.s2_ref, f32[136,128]{1,0:T(8,128)S(1)} %collective-permute-done.1.small_ref, bf16[128,2048]{1,0:T(8,128)(2,1)S(1)} %get-tuple-element.20.bm_ref, bf16[1536,128]{1,0:T(8,128)(2,1)S(1)} %get-tuple-element.25.pl_ref, ...), custom_call_target="tpu_custom_call" | custom-call | flops 1000000000 | bytes 4468740 | tf_op jit(solution)/shard_map/pallas_call | solution.py:438
Async XLA Ops:
  0.0 32.4 %copy-start.1 = (bf16[512,256]{1,0:T(8,128)(2,1)S(1)}, bf16[512,256]{1,0:T(8,128)(2,1)}, u32[]{:S(2)}) copy-start(bf16[512,256]{1,0:T(8,128)(2,1)} %constant.8.clone.sel_hbm.sel_ref) | copy-start | bytes 786436
  0.0 32.4 %copy-start.2 = (s32[256,8]{0,1:T(8,128)S(1)}, s32[256,8]{0,1:T(8,128)}, u32[]{:S(2)}) copy-start(s32[256,8]{0,1:T(8,128)} %param.16) | copy-start | bytes 24580
  0.0 32.4 %copy-start.3 = (f32[1,256,512]{2,1,0:T(8,128)S(1)}, f32[1,256,512]{2,1,0:T(8,128)}, u32[]{:S(2)}) copy-start(f32[1,256,512]{2,1,0:T(8,128)} %param.12) | copy-start | bytes 1572868
  0.0 32.4 %copy-start.4 = (f32[256,512]{1,0:T(8,128)S(1)}, f32[256,512]{1,0:T(8,128)}, u32[]{:S(2)}) copy-start(f32[256,512]{1,0:T(8,128)} %met_ref.1) | copy-start | bytes 1572868
  0.0 32.4 %copy-start.5 = (s32[256,6]{0,1:T(8,128)S(1)}, s32[256,6]{0,1:T(8,128)}, u32[]{:S(2)}) copy-start(s32[256,6]{0,1:T(8,128)} %param.15) | copy-start | bytes 18436
  0.0 32.4 %copy-start.6 = (f32[8,512]{1,0:T(8,128)S(1)}, f32[8,512]{1,0:T(8,128)}, u32[]{:S(2)}) copy-start(f32[8,512]{1,0:T(8,128)} %constant.6.clone.bas_hbm.bas_ref) | copy-start | bytes 49156
  0.0 32.4 %copy-start.7 = (f32[8,128]{1,0:T(8,128)S(1)}, f32[8,128]{1,0:T(8,128)}, u32[]{:S(2)}) copy-start(f32[8,128]{1,0:T(8,128)} %constant.7.clone.pair_hbm.pair_ref) | copy-start | bytes 12292
  32.5 38.4 %copy-start = (f32[1,2,256,512]{3,2,1,0:T(8,128)S(1)}, f32[1,2,256,512]{3,2,1,0:T(8,128)}, u32[]{:S(2)}) copy-start(f32[1,2,256,512]{3,2,1,0:T(8,128)} %param.11) | copy-start | bytes 3145732
  39.1 31.8 %collective-permute-start = (f32[512,512]{1,0:T(8,128)S(1)}, f32[512,512]{1,0:T(8,128)S(1)}, u32[]{:S(2)}, u32[]{:S(2)}) collective-permute-start(f32[512,512]{1,0:T(8,128)S(1)} %get-tuple-element.27), channel_id=1, source_target_pairs={{0,8},{8,16},{16,24},{24,32},{32,40},{40,48},{48,56},{56,64},{64,7... | collective-permute-start | bytes 3145736 | tf_op jit(solution)/shard_map/ppermute | solution.py:496
  65.2 5.6 %collective-permute-start.1 = (f32[136,128]{1,0:T(8,128)S(1)}, f32[136,128]{1,0:T(8,128)S(1)}, u32[]{:S(2)}, u32[]{:S(2)}) collective-permute-start(f32[136,128]{1,0:T(8,128)S(1)} %shard_map.111), channel_id=1, source_target_pairs={{0,8},{8,16},{16,24},{24,32},{32,40},{40,48},{48,56},{56,64},{64,7... | collective-permute-start | bytes 208904 | tf_op jit(solution)/shard_map/ppermute | solution.py:498

commit v2 on v1

--- a/solution.py
+++ b/solution.py
@@ -17,7 +17,6 @@
 HALO = 2 * SHARED
 INNER_TOP = 768
 MSG1 = 88
-MSG2 = 72
 FACE_CORNERS = (
     (0, 1, 2, 3),
     (4, 5, 6, 7),
@@ -357,7 +356,7 @@
 def second_kernel(
     s1_ref, got_ref, p_ref, bm_ref, bh_ref, bl_ref, kh_ref, kl_ref, pl_ref, lb_ref, swl_ref, met_ref, fs_ref, cor_ref,
     sel_ref, bas_ref, pair_ref,
-    out_ref, msg_ref, q_ref, g_ref,
+    out_ref, msg_ref, near_ref, q_ref, g_ref,
 ):
     me = lax.axis_index("dom")
     before, after = lax.rem(me + 7, 8), lax.rem(me + 1, 8)
@@ -398,48 +397,76 @@
     for r in range(4):
         low_hot = hot(mine[4 + r : 5 + r, :] == which)
         coarse = coarse + deposit(eight(rf[r : r + 1, :], rf[4 + r : 5 + r, :]), mine[r : r + 1, :], low_hot)
-    send_rows(msg_ref, me, coarse, yh + yl)
-
-
-def pack_kernel(got_ref, kh_ref, kl_ref, out_ref):
+    rows = yh + yl
+    even = (me & 1) == 0
+    near_ref[...] = jnp.where(even, rows[SHARED:], rows[:SHARED])
+    far = jnp.where(even, rows[:SHARED], rows[SHARED:])
+    for j in range(4):
+        msg_ref[j, 0:8, :] = coarse
+        msg_ref[j, 8:, :] = far
+
+
+def pack_kernel(got_ref, near_ref, sum_ref, across_ref):
     me = lax.axis_index("dom")
     coarse = got_ref[0, 0:8, :]
-    for j in range(1, 8):
+    for j in range(1, 4):
         coarse = coarse + got_ref[j, 0:8, :]
-    out_ref[0:8, :] = solve(coarse, kh_ref[...], kl_ref[...])
-    out_ref[8 : 8 + SHARED, :] = got_ref[lax.rem(me + 7, 8), 8:MSG2, :]
-    out_ref[8 + SHARED :, :] = got_ref[lax.rem(me + 1, 8), 8:MSG2, :]
-
-
-def last_kernel(tan_ref, s2_ref, small_ref, bm_ref, pl_ref, lb_ref, cor_ref, sel_ref, ang_ref, out_ref):
+    sum_ref[...] = coarse
+    across_ref[0:8, :] = coarse
+    across_ref[8 : 8 + SHARED, :] = near_ref[...]
+    giver = (me // 2 + jnp.where((me & 1) == 0, 1, 3)) & 3
+    across_ref[8 + SHARED :, :] = got_ref[giver, 8:, :]
+
+
+def prepare_kernel(lb_ref, cor_ref, fs_ref, ang_ref, bm_ref, bas_ref, pl_ref, sel_ref, turn_ref):
+    angle = jnp.where(lax.axis_index("seg") == 0, ang_ref[0], F32(0.0))
+    angles = jnp.full((8, 128), angle, F32)
+    turn_ref[0:8, :] = jnp.cos(angles)
+    turn_ref[8:16, :] = jnp.sin(angles)
+    _, cvl = corner_parts(cor_ref)
+    bm_ref[...] = hot(row_of(cvl) == iota((128, 1), 0).astype(F32))
+    bas_ref[...] = lb_ref[:, :NODES]
+    columns = slot_columns(fs_ref)
+    target = shared_target_row()
+    for f in range(FACES):
+        pl_ref[f * ELEMS : (f + 1) * ELEMS, :] = hot(columns[f] == target)
+    lane = iota((1, 4 * PLANE), 1)
+    face, p, q = lane >> 6, (lane >> 3) & 7, lane & 7
+    middle = p * PLANE + q + jnp.where(face == 1, 56, 0)
+    outer = p * PLANE + q * 8 + jnp.where(face == 3, 7, 0)
+    sel_ref[...] = hot(iota((NODES, 1), 0) == jnp.where(face < 2, middle, outer))
+
+
+def last_kernel(
+    tan_ref, s2_ref, sum_ref, across_ref, kh_ref, kl_ref, bm_ref, bas_ref, pl_ref, sel_ref, cor_ref, turn_ref,
+    out_ref,
+):
+    even = (lax.axis_index("dom") & 1) == 0
+    near, far = across_ref[8 : 8 + SHARED, :], across_ref[8 + SHARED :, :]
+    arrived = jnp.concatenate([jnp.where(even, far, near), jnp.where(even, near, far)], axis=0)
+    partly = s2_ref[...] + F32(0.5) * halo_part(pl_ref[...], arrived, sel_ref[...])
     cvh, _ = corner_parts(cor_ref)
-    corners = corner_values(small_ref[0:8, :], row_of(cvh), bm_ref[...])
-    state = (
-        s2_ref[...]
-        + F32(0.5) * halo_part(pl_ref[...], small_ref[8:, :], sel_ref[...])
-        - dot_tn(corners, lb_ref[:, :NODES])
-    )
-    angle = jnp.where(lax.axis_index("seg") == 0, ang_ref[0], F32(0.0))
-    angles = jnp.full((1, NODES), angle, F32)
-    cosine, sine = jnp.cos(angles), jnp.sin(angles)
+    solved = solve(sum_ref[...] + across_ref[0:8, :], kh_ref[...], kl_ref[...])
+    state = partly - dot_tn(corner_values(solved, row_of(cvh), bm_ref[...]), bas_ref[...])
+    cosine = jnp.concatenate([turn_ref[0:1, :]] * 4, axis=1)
+    sine = jnp.concatenate([turn_ref[8:9, :]] * 4, axis=1)
     re, im = state[:ELEMS], state[ELEMS:]
     out_ref[0:ELEMS, :] = tan_ref[0:ELEMS, :] - (cosine * re - sine * im)
     out_ref[ELEMS:, :] = tan_ref[ELEMS:, :] - (sine * re + cosine * im)
 
 
 VMEM = pl.BlockSpec(memory_space=pltpu.VMEM)
-SMEM = pl.BlockSpec(memory_space=pltpu.SMEM)
 HBM = pl.BlockSpec(memory_space=pltpu.HBM)
 
 
-def call(body, outs, scratch, ins, flops, specs=None, limit=28):
+def call(body, outs, scratch, ins, flops, specs=None, outs_at=None, limit=28):
     size = sum(int(np.prod(o.shape)) * o.dtype.itemsize for o in outs)
     size += sum(int(np.prod(a.shape)) * a.dtype.itemsize for a in ins)
     return pl.pallas_call(
         body,
         out_shape=outs,
         in_specs=specs or [VMEM] * len(ins),
-        out_specs=[VMEM] * len(outs),
+        out_specs=outs_at or [VMEM] * len(outs),
         scratch_shapes=scratch,
         compiler_params=pltpu.CompilerParams(vmem_limit_bytes=limit * 1024 * 1024),
         cost_estimate=pl.CostEstimate(flops=flops, bytes_accessed=size, transcendentals=0),
@@ -477,32 +504,52 @@
             like(count, HALO, dtype=BF16),
             like(32, 2 * NODES, dtype=BF16),
         ],
-        [faces, faces] + [pltpu.VMEM(a.shape, a.dtype) for a in ins] + [pltpu.SemaphoreType.DMA((len(ins),))],
+        [faces, faces]
+        + [pltpu.VMEM(a.shape, a.dtype) for a in ins]
+        + [pltpu.SemaphoreType.DMA((len(ins),))],
         [pltpu.with_memory_space_constraint(a, pltpu.HBM) for a in ins],
         4_000_000_000,
         [HBM] * len(ins),
     )
     got = lax.all_to_all(msg, "dom", 0, 0)
-    s2, msg = call(
+    s2, msg, near = call(
         second_kernel,
-        [field, like(8, MSG2, 128)],
+        [field, like(4, 8 + SHARED, 128), like(SHARED, 128)],
         [faces, faces],
         [s1, got, p, bm, bh, bl, kh, kl, placed, lb, swirl, metric, slots, ids, select, basis, pair],
         4_000_000_000,
     )
     size = lax.axis_size("seg")
     ring = [(i, (i + 1) % size) for i in range(size)]
-    got = lax.all_to_all(msg, "dom", 0, 0)
+
+    def onward(target):
+        return [(8 * i + d, 8 * j + target(d)) for i, j in ring for d in range(8)]
+
     s2 = lax.ppermute(s2, "seg", ring)
-    (small,) = call(pack_kernel, [like(8 + HALO, 128)], [], [got, kh, kl], 100_000_000)
-    small = lax.ppermute(small, "seg", ring)
+    got = lax.all_to_all(msg, "dom", 0, 0, axis_index_groups=[[0, 2, 4, 6], [1, 3, 5, 7]])
+    total, across = call(pack_kernel, [like(8, 128), like(8 + HALO, 128)], [], [got, near], 1_000_000)
+    across = lax.ppermute(across, ("seg", "dom"), onward(lambda d: d ^ 1))
+    total = lax.ppermute(total, "seg", ring)
+    bm, wide, placed, select, turn = call(
+        prepare_kernel,
+        [
+            like(128, 8 * ELEMS, dtype=BF16),
+            like(32, NODES, dtype=BF16),
+            like(count, HALO, dtype=BF16),
+            like(NODES, 4 * PLANE, dtype=BF16),
+            like(16, 128),
+        ],
+        [],
+        [lb, ids, slots, phase_angle],
+        1_000_000_000,
+        [VMEM] * 3 + [pl.BlockSpec(memory_space=pltpu.SMEM)],
+    )
     (out,) = call(
         last_kernel,
         [field],
         [],
-        [state, s2, small, bm, placed, lb, ids, select, phase_angle],
+        [state, s2, total, across, kh, kl, bm, wide, placed, select, ids, turn],
         1_000_000_000,
-        [VMEM] * 8 + [SMEM],
     )
     return out.reshape(1, 2, ELEMS, NODES)
 

time: 73.3 us -> 66.4 us (0.906)
  the two profiles are of different devices: /device:TPU:200 before, /device:TPU:256 now
where the time goes in v2:
time: 66.4 us; the launch traced here: 66.1 us
  blocking collectives  23.6 us (36%)
  Pallas kernels  18.6 us (28%)
  starting transfers between devices  11.7 us (18%)
  waiting for transfers between devices  11.3 us (17%)
  between operations  0.77 us (1%)
    all_to_all x1, blocking collectives, shards(): got = lax.all_to_all(msg, 'dom', 0, 0)  23.6 us
    pallas_call x5, Pallas kernels, call(): pl.pallas_call(body, out_shape=outs, in_specs=specs or [VMEM] * len(ins),...  18.6 us
    ppermute x1, waiting for transfers between devices, shards(): total = lax.ppermute(total, 'seg', ring)  5.95 us
    all_to_all x1, waiting for transfers between devices, shards(): lax.all_to_all(msg, 'dom', 0, 0, axis_index_groups=[[0, 2, 4, 6], [1, 3,...  5.38 us
    ppermute x1, starting transfers between devices, shards(): across = lax.ppermute(across, ('seg', 'dom'), onward(lambda d: d ^ 1))  3.98 us
    all_to_all x1, starting transfers between devices, shards(): lax.all_to_all(msg, 'dom', 0, 0, axis_index_groups=[[0, 2, 4, 6], [1, 3,...  3.35 us
    ppermute x1, starting transfers between devices, shards(): total = lax.ppermute(total, 'seg', ring)  2.31 us
    ppermute x1, starting transfers between devices, shards(): s2 = lax.ppermute(s2, 'seg', ring)  2.04 us
  transfers between devices with their start and end apart: 4, of which 2 were waited for; matrix products, arithmetic and copies ran while one was open for 0% of the time, Pallas kernels for 1%

profile of v2, /device:TPU:256, one launch (start us, length us, event | category | flops | bytes accessed | tf_op | source)
XLA Modules:
  0.0 66.1 jit_solution(7762347933689039575)
XLA Ops:
  0.0 0.0 copy-start.1
  0.0 0.0 copy-start.2
  0.0 0.0 copy-start.3
  0.0 0.0 copy-start.4
  0.0 0.0 copy-start.5
  0.0 0.0 copy-start.6
  0.0 0.0 copy-start.7
  0.1 7.7 %shard_map.109 = (f32[512,512]{1,0:T(8,128)S(1)}, f32[8,88,128]{2,1,0:T(8,128)S(1)}, bf16[1536,1536]{1,0:T(8,128)(2,1)S(1)}, bf16[128,2048]{1,0:T(8,128)(2,1)S(1...) custom-call(f32[512,512]{1,0:T(8,128)} %bitcast.5, ...), custom_call_target="tpu_custom_call" | custom-call | flops 4000000000 | bytes 12650752 | tf_op jit(solution)/shard_map/pallas_call | solution.py:465
  7.8 23.6 %all_to_all.10.got_ref = f32[8,88,128]{2,1,0:T(8,128)S(1)} all-to-all(f32[8,88,128]{2,1,0:T(8,128)S(1)} %get-tuple-element.26), channel_id=1, replica_groups=mesh['seg'=64,'dom'=8] {'dom'}, dimensions={0} | all-to-all | bytes 720896 | tf_op jit(solution)/shard_map/all_to_all | solution.py:514
  31.4 0.0 copy-done.1
  31.4 0.0 copy-done.2
  31.4 0.0 copy-done.3
  31.4 0.0 copy-done.4
  31.4 0.0 copy-done.5
  31.4 0.0 copy-done.6
  31.4 0.0 copy-done.7
  31.4 7.3 %shard_map.110 = (f32[512,512]{1,0:T(8,128)}, f32[4,72,128]{2,1,0:T(8,128)}, f32[64,128]{1,0:T(8,128)S(1)}) custom-call(f32[512,512]{1,0:T(8,128)S(1)} %get-tuple-element.25.s1_ref, f32[8,88,128]{2,1,0:T(8,128)S(1)} %all_to_all.10.got_ref, bf16[1536,1536]{1,0:T(8,128)(2,1)S(1)} %get-tuple-element.27.p_ref, bf16[128,2048]{1,0:T(8,128)(2,1)S(1)} %get-tuple-element.28.bm_ref, ...), custom_call_target="tpu_custom_call" | custom-call | flops 4000000000 | bytes 11782144 | tf_op jit(solution)/shard_map/pallas_call | solution.py:465
  38.8 0.0 copy-start
  38.8 2.0 %collective-permute-start = (f32[512,512]{1,0:T(8,128)}, f32[512,512]{1,0:T(8,128)S(1)}, u32[]{:S(2)}, u32[]{:S(2)}) collective-permute-start(f32[512,512]{1,0:T(8,128)} %get-tuple-element.35), channel_id=1, source_target_pairs={{0,8},{8,16},{16,24},{24,32},{32,40},{40,48},{48,56},{56,64},{64,7... | collective-permute-start | bytes 3145736 | tf_op jit(solution)/shard_map/ppermute | solution.py:528
  40.8 3.3 %all-to-all-start.1 = ((f32[4,72,128]{2,1,0:T(8,128)}), f32[4,72,128]{2,1,0:T(8,128)S(1)}, u32[]{:S(2)}, u32[]{:S(2)}) async-start(f32[4,72,128]{2,1,0:T(8,128)} %get-tuple-element.36), calls=%async_computation.1 | async-start | bytes 294912 | tf_op jit(solution)/shard_map/all_to_all | solution.py:529
  44.8 5.4 %all-to-all-done.1.got_ref = f32[4,72,128]{2,1,0:T(8,128)S(1)} async-done(((f32[4,72,128]{2,1,0:T(8,128)}), f32[4,72,128]{2,1,0:T(8,128)S(1)}, u32[]{:S(2)}, u32[]{:S(2)}) %all-to-all-start.1) | async-done | bytes 147488 | tf_op jit(solution)/shard_map/all_to_all | solution.py:529
  50.2 4.0 %collective-permute-start.2 = (f32[136,128]{1,0:T(8,128)S(1)}, f32[136,128]{1,0:T(8,128)S(1)}, u32[]{:S(2)}, u32[]{:S(2)}) collective-permute-start(f32[136,128]{1,0:T(8,128)S(1)} %get-tuple-element.39), channel_id=1, source_target_pairs={{0,9},{1,8},{2,11},{3,10},{4,13},{5,12},{6,15},{7,14},{8,17},{9,16... | collective-permute-start | bytes 208904 | tf_op jit(solution)/shard_map/ppermute | solution.py:531
  54.2 2.3 %collective-permute-start.1 = (f32[8,128]{1,0:T(8,128)S(1)}, f32[8,128]{1,0:T(8,128)S(1)}, u32[]{:S(2)}, u32[]{:S(2)}) collective-permute-start(f32[8,128]{1,0:T(8,128)S(1)} %get-tuple-element.38), channel_id=1, source_target_pairs={{0,8},{8,16},{16,24},{24,32},{32,40},{40,48},{48,56},{56,64},{64,7... | collective-permute-start | bytes 12296 | tf_op jit(solution)/shard_map/ppermute | solution.py:532
  56.5 0.6 shard_map.112
  57.1 6.0 %collective-permute-done.1.sum_ref = f32[8,128]{1,0:T(8,128)S(1)} collective-permute-done((f32[8,128]{1,0:T(8,128)S(1)}, f32[8,128]{1,0:T(8,128)S(1)}, u32[]{:S(2)}, u32[]{:S(2)}) %collective-permute-start.1) | collective-permute-done | bytes 4128 | tf_op jit(solution)/shard_map/ppermute | solution.py:532
  63.0 0.0 collective-permute-done.2.across_ref
  63.0 0.0 collective-permute-done.s2_ref
  63.0 0.0 copy-done
  63.0 3.0 %shard_map.113 = f32[512,512]{1,0:T(8,128)} custom-call(f32[512,512]{1,0:T(8,128)S(1)} %bitcast.6, f32[512,512]{1,0:T(8,128)S(1)} %collective-permute-done.s2_ref, f32[8,128]{1,0:T(8,128)S(1)} %collective-permute-done.1.sum_ref, f32[136,128]{1,0:T(8,128)S(1)} %collective-permute-done.2.across_ref, bf16[512,512]{1,0:T(8,128)(2,1)S(1)} %get-tuple-element.31.kh_ref, ...), custom_call_target="tpu_custom_call" | custom-call | flops 1000000000 | bytes 5496832 | tf_op jit(solution)/shard_map/pallas_call | solution.py:465
  (1 shorter events, 0.0 us)
Async XLA Ops:
  0.0 31.4 %copy-start.1 = (s32[256,8]{0,1:T(8,128)S(1)}, s32[256,8]{0,1:T(8,128)}, u32[]{:S(2)}) copy-start(s32[256,8]{0,1:T(8,128)} %param.16) | copy-start | bytes 24580
  0.0 31.4 %copy-start.2 = (f32[1,256,512]{2,1,0:T(8,128)S(1)}, f32[1,256,512]{2,1,0:T(8,128)}, u32[]{:S(2)}) copy-start(f32[1,256,512]{2,1,0:T(8,128)} %param.12) | copy-start | bytes 1572868
  0.0 31.4 %copy-start.3 = (f32[256,512]{1,0:T(8,128)S(1)}, f32[256,512]{1,0:T(8,128)}, u32[]{:S(2)}) copy-start(f32[256,512]{1,0:T(8,128)} %met_ref.1) | copy-start | bytes 1572868
  0.0 31.4 %copy-start.4 = (s32[256,6]{0,1:T(8,128)S(1)}, s32[256,6]{0,1:T(8,128)}, u32[]{:S(2)}) copy-start(s32[256,6]{0,1:T(8,128)} %param.15) | copy-start | bytes 18436
  0.0 31.4 %copy-start.5 = (bf16[512,256]{1,0:T(8,128)(2,1)S(1)}, bf16[512,256]{1,0:T(8,128)(2,1)}, u32[]{:S(2)}) copy-start(bf16[512,256]{1,0:T(8,128)(2,1)} %constant.8.clone.sel_hbm.sel_ref) | copy-start | bytes 786436
  0.0 31.4 %copy-start.6 = (f32[8,512]{1,0:T(8,128)S(1)}, f32[8,512]{1,0:T(8,128)}, u32[]{:S(2)}) copy-start(f32[8,512]{1,0:T(8,128)} %constant.6.clone.bas_hbm.bas_ref) | copy-start | bytes 49156
  0.0 31.4 %copy-start.7 = (f32[8,128]{1,0:T(8,128)S(1)}, f32[8,128]{1,0:T(8,128)}, u32[]{:S(2)}) copy-start(f32[8,128]{1,0:T(8,128)} %constant.7.clone.pair_hbm.pair_ref) | copy-start | bytes 12292
  38.8 24.3 %copy-start = (f32[1,2,256,512]{3,2,1,0:T(8,128)S(1)}, f32[1,2,256,512]{3,2,1,0:T(8,128)}, u32[]{:S(2)}) copy-start(f32[1,2,256,512]{3,2,1,0:T(8,128)} %param.11) | copy-start | bytes 3145732
  38.8 24.3 %collective-permute-start = (f32[512,512]{1,0:T(8,128)}, f32[512,512]{1,0:T(8,128)S(1)}, u32[]{:S(2)}, u32[]{:S(2)}) collective-permute-start(f32[512,512]{1,0:T(8,128)} %get-tuple-element.35), channel_id=1, source_target_pairs={{0,8},{8,16},{16,24},{24,32},{32,40},{40,48},{48,56},{56,64},{64,7... | collective-permute-start | bytes 3145736 | tf_op jit(solution)/shard_map/ppermute | solution.py:528
  40.8 9.4 %all-to-all-start.1 = ((f32[4,72,128]{2,1,0:T(8,128)}), f32[4,72,128]{2,1,0:T(8,128)S(1)}, u32[]{:S(2)}, u32[]{:S(2)}) async-start(f32[4,72,128]{2,1,0:T(8,128)} %get-tuple-element.36), calls=%async_computation.1 | async-start | bytes 294912 | tf_op jit(solution)/shard_map/all_to_all | solution.py:529
  50.2 12.8 %collective-permute-start.2 = (f32[136,128]{1,0:T(8,128)S(1)}, f32[136,128]{1,0:T(8,128)S(1)}, u32[]{:S(2)}, u32[]{:S(2)}) collective-permute-start(f32[136,128]{1,0:T(8,128)S(1)} %get-tuple-element.39), channel_id=1, source_target_pairs={{0,9},{1,8},{2,11},{3,10},{4,13},{5,12},{6,15},{7,14},{8,17},{9,16... | collective-permute-start | bytes 208904 | tf_op jit(solution)/shard_map/ppermute | solution.py:531
  54.2 8.8 %collective-permute-start.1 = (f32[8,128]{1,0:T(8,128)S(1)}, f32[8,128]{1,0:T(8,128)S(1)}, u32[]{:S(2)}, u32[]{:S(2)}) collective-permute-start(f32[8,128]{1,0:T(8,128)S(1)} %get-tuple-element.38), channel_id=1, source_target_pairs={{0,8},{8,16},{16,24},{24,32},{32,40},{40,48},{48,56},{56,64},{64,7... | collective-permute-start | bytes 12296 | tf_op jit(solution)/shard_map/ppermute | solution.py:532

commit v3 on v2

--- a/solution.py
+++ b/solution.py
@@ -244,15 +244,19 @@
     return jnp.where(s < SHARED, s, s + (INNER_TOP - SHARED)).astype(F32)
 
 
-def halo_part(placed, arrived, select):
+def halo_faces(placed, arrived):
     high, low = split(arrived)
     both = jnp.concatenate([high.astype(F32), low.astype(F32)], axis=1).astype(BF16)
-    got = dot(placed, both)
+    return dot(placed, both)
+
+
+def halo_part(placed, arrived, select):
+    got = halo_faces(placed, arrived)
     return scattered([got[f * ELEMS : (f + 1) * ELEMS] for f in range(FACES)], select)
 
 
 def settle(advanced, partner, select):
-    blocks = [partner[f * ELEMS : (f + 1) * ELEMS].astype(F32) for f in range(FACES)]
+    blocks = [partner[f * ELEMS : (f + 1) * ELEMS] for f in range(FACES)]
     kept = advanced * (F32(1.0) - F32(0.5) * multiplicity())
     return kept + F32(0.5) * scattered(blocks, select)
 
@@ -276,8 +280,8 @@
 
 def first_kernel(
     tan_hbm, swl_hbm, met_hbm, sti_hbm, fs_hbm, cor_hbm, sel_hbm, bas_hbm, pair_hbm, inv_hbm,
-    out_ref, msg_ref, p_ref, bm_ref, bh_ref, bl_ref, kh_ref, kl_ref, pl_ref, lb_ref,
-    q_ref, g_ref, tan_ref, swl_ref, met_ref, sti_ref, fs_ref, cor_ref, sel_ref, bas_ref, pair_ref, inv_ref, sems,
+    adv_ref, g_ref, msg_ref, p_ref, bm_ref, bh_ref, bl_ref, kh_ref, kl_ref, pl_ref, lb_ref,
+    q_ref, tan_ref, swl_ref, met_ref, sti_ref, fs_ref, cor_ref, sel_ref, bas_ref, pair_ref, inv_ref, sems,
 ):
     me = lax.axis_index("dom")
     moves = [
@@ -331,30 +335,31 @@
     target = shared_target_row()
     for f in range(FACES):
         pl_ref[f * ELEMS : (f + 1) * ELEMS, :] = hot(columns[f] == target)
-    for move in moves[3:]:
+    for move in moves[3:9]:
         move.wait()
     basis = bas_ref[...]
     stiff = stiff_of(jnp.concatenate([basis, basis], axis=0), bh_ref[...], bl_ref[...])
     lb_ref[:, :NODES] = tripled(basis)
     lb_ref[:, NODES:] = tripled(stiff[:8])
-    kh, kl = split(inv_ref[...])
-    kh_ref[...] = kh
-    kl_ref[...] = kl
 
     state = tan_ref[...]
     advanced = advance(state, stiff_of(state, bh_ref[...], bl_ref[...]), met_ref[...], swl_ref[...])
+    adv_ref[...] = advanced
     blocks, ah, al = face_blocks(advanced, sel_ref[...])
     pair_up(blocks, p_ref, q_ref, g_ref)
-    out_ref[...] = settle(advanced, g_ref[...], sel_ref[...])
     coarse = coarse_of(ah, al, g_ref[...], bas_ref[...], pair_ref[...], cvh, bm_ref[...])
     y = dot(shared, q_ref[...])
     yh, yl = y[:, :HALO], y[:, HALO:]
     rf = two_products(pair_ref[...] * F32(0.5 / NODES), yh.astype(BF16), yl.astype(BF16))
     send_rows(msg_ref, me, jnp.concatenate([coarse, rf, ids], axis=0), yh + yl)
+    moves[9].wait()
+    kh, kl = split(inv_ref[...])
+    kh_ref[...] = kh
+    kl_ref[...] = kl
 
 
 def second_kernel(
-    s1_ref, got_ref, p_ref, bm_ref, bh_ref, bl_ref, kh_ref, kl_ref, pl_ref, lb_ref, swl_ref, met_ref, fs_ref, cor_ref,
+    adv_ref, g1_ref, got_ref, p_ref, bm_ref, bh_ref, bl_ref, kh_ref, kl_ref, pl_ref, lb_ref, swl_ref, met_ref, fs_ref, cor_ref,
     sel_ref, bas_ref, pair_ref,
     out_ref, msg_ref, near_ref, q_ref, g_ref,
 ):
@@ -366,7 +371,8 @@
     which = iota((128, 1), 0).astype(F32)
 
     arrived = jnp.concatenate([got_ref[before, 24:MSG1, :], got_ref[after, 24:MSG1, :]], axis=0)
-    partly = s1_ref[...] + F32(0.5) * halo_part(pl_ref[...], arrived, select)
+    partner = g1_ref[...].astype(F32) + halo_faces(pl_ref[...], arrived)
+    partly = settle(adv_ref[...], partner, select)
     stiff = stiff_of(partly, bh_ref[...], bl_ref[...])
 
     coarse = got_ref[0, 0:8, :]
@@ -387,7 +393,7 @@
     advanced = advance(partly - both[:, :NODES], stiff - both[:, NODES:], met_ref[...], swl_ref[...])
     blocks, ah, al = face_blocks(advanced, select)
     pair_up(blocks, p_ref, q_ref, g_ref)
-    out_ref[...] = settle(advanced, g_ref[...], select)
+    out_ref[...] = settle(advanced, g_ref[...].astype(F32), select)
     coarse = coarse_of(ah, al, g_ref[...], bas_ref[...], pair_ref[...], cvh, bm_ref[...])
     shared = hot(shared_target_column() == jnp.concatenate(slot_rows(fs_ref), axis=1))
     y = dot(shared, q_ref[...])
@@ -490,10 +496,11 @@
     faces = pltpu.VMEM((count, 2 * HALO), BF16)
 
     ins = [state, swirl, metric, stiffness, slots, ids, select, basis, pair, coarse_inverse]
-    s1, msg, p, bm, bh, bl, kh, kl, placed, lb = call(
+    advanced, g, msg, p, bm, bh, bl, kh, kl, placed, lb = call(
         first_kernel,
         [
             field,
+            like(count, 2 * HALO, dtype=BF16),
             like(8, MSG1, 128),
             like(count, count, dtype=BF16),
             like(128, 8 * ELEMS, dtype=BF16),
@@ -504,7 +511,7 @@
             like(count, HALO, dtype=BF16),
             like(32, 2 * NODES, dtype=BF16),
         ],
-        [faces, faces]
+        [faces]
         + [pltpu.VMEM(a.shape, a.dtype) for a in ins]
         + [pltpu.SemaphoreType.DMA((len(ins),))],
         [pltpu.with_memory_space_constraint(a, pltpu.HBM) for a in ins],
@@ -516,7 +523,7 @@
         second_kernel,
         [field, like(4, 8 + SHARED, 128), like(SHARED, 128)],
         [faces, faces],
-        [s1, got, p, bm, bh, bl, kh, kl, placed, lb, swirl, metric, slots, ids, select, basis, pair],
+        [advanced, g, got, p, bm, bh, bl, kh, kl, placed, lb, swirl, metric, slots, ids, select, basis, pair],
         4_000_000_000,
     )
     size = lax.axis_size("seg")

time: 66.4 us -> 65.9 us (level)
  no operation moved by 1% of the time
where the time goes in v3:
time: 65.9 us; the launch traced here: 65.6 us
  blocking collectives  23.6 us (36%)
  Pallas kernels  18.1 us (27%)
  starting transfers between devices  11.7 us (18%)
  waiting for transfers between devices  11.3 us (17%)
  between operations  0.77 us (1%)
    all_to_all x1, blocking collectives, shards(): got = lax.all_to_all(msg, 'dom', 0, 0)  23.6 us
    pallas_call x5, Pallas kernels, call(): pl.pallas_call(body, out_shape=outs, in_specs=specs or [VMEM] * len(ins),...  18.1 us
    ppermute x1, waiting for transfers between devices, shards(): total = lax.ppermute(total, 'seg', ring)  5.95 us
    all_to_all x1, waiting for transfers between devices, shards(): lax.all_to_all(msg, 'dom', 0, 0, axis_index_groups=[[0, 2, 4, 6], [1, 3,...  5.38 us
    ppermute x1, starting transfers between devices, shards(): across = lax.ppermute(across, ('seg', 'dom'), onward(lambda d: d ^ 1))  3.98 us
    all_to_all x1, starting transfers between devices, shards(): lax.all_to_all(msg, 'dom', 0, 0, axis_index_groups=[[0, 2, 4, 6], [1, 3,...  3.35 us
    ppermute x1, starting transfers between devices, shards(): total = lax.ppermute(total, 'seg', ring)  2.31 us
    ppermute x1, starting transfers between devices, shards(): s2 = lax.ppermute(s2, 'seg', ring)  2.04 us
  transfers between devices with their start and end apart: 4, of which 2 were waited for; matrix products, arithmetic and copies ran while one was open for 0% of the time, Pallas kernels for 1%

profile of v3, /device:TPU:256, one launch (start us, length us, event | category | flops | bytes accessed | tf_op | source)
XLA Modules:
  0.0 65.6 jit_solution(6486743004171989344)
XLA Ops:
  0.0 0.0 copy-start.1
  0.0 0.0 copy-start.2
  0.0 0.0 copy-start.3
  0.0 0.0 copy-start.4
  0.0 0.0 copy-start.5
  0.0 0.0 copy-start.6
  0.0 0.0 copy-start.7
  0.1 7.2 %shard_map.109 = (f32[512,512]{1,0:T(8,128)S(1)}, bf16[1536,256]{1,0:T(8,128)(2,1)S(1)}, f32[8,88,128]{2,1,0:T(8,128)S(1)}, bf16[1536,1536]{1,0:T(8,128)(2,1)S(1...) custom-call(f32[512,512]{1,0:T(8,128)} %bitcast.5, ...), custom_call_target="tpu_custom_call" | custom-call | flops 4000000000 | bytes 13437184 | tf_op jit(solution)/shard_map/pallas_call | solution.py:471
  7.2 23.6 %all_to_all.10.got_ref = f32[8,88,128]{2,1,0:T(8,128)S(1)} all-to-all(f32[8,88,128]{2,1,0:T(8,128)S(1)} %get-tuple-element.28), channel_id=1, replica_groups=mesh['seg'=64,'dom'=8] {'dom'}, dimensions={0} | all-to-all | bytes 720896 | tf_op jit(solution)/shard_map/all_to_all | solution.py:521
  30.9 0.0 copy-done.1
  30.9 0.0 copy-done.2
  30.9 0.0 copy-done.3
  30.9 0.0 copy-done.4
  30.9 0.0 copy-done.5
  30.9 0.0 copy-done.6
  30.9 0.0 copy-done.7
  30.9 7.3 %shard_map.110 = (f32[512,512]{1,0:T(8,128)}, f32[4,72,128]{2,1,0:T(8,128)}, f32[64,128]{1,0:T(8,128)S(1)}) custom-call(f32[512,512]{1,0:T(8,128)S(1)} %get-tuple-element.26.adv_ref, bf16[1536,256]{1,0:T(8,128)(2,1)S(1)} %get-tuple-element.27.g1_ref, f32[8,88,128]{2,1,0:T(8,128)S(1)} %all_to_all.10.got_ref, bf16[1536,1536]{1,0:T(8,128)(2,1)S(1)} %get-tuple-element.29.p_ref, ...), custom_call_target="tpu_custom_call" | custom-call | flops 4000000000 | bytes 12568576 | tf_op jit(solution)/shard_map/pallas_call | solution.py:471
  38.2 0.0 copy-start
  38.2 2.0 %collective-permute-start = (f32[512,512]{1,0:T(8,128)}, f32[512,512]{1,0:T(8,128)S(1)}, u32[]{:S(2)}, u32[]{:S(2)}) collective-permute-start(f32[512,512]{1,0:T(8,128)} %get-tuple-element.37), channel_id=1, source_target_pairs={{0,8},{8,16},{16,24},{24,32},{32,40},{40,48},{48,56},{56,64},{64,7... | collective-permute-start | bytes 3145736 | tf_op jit(solution)/shard_map/ppermute | solution.py:535
  40.3 3.3 %all-to-all-start.1 = ((f32[4,72,128]{2,1,0:T(8,128)}), f32[4,72,128]{2,1,0:T(8,128)S(1)}, u32[]{:S(2)}, u32[]{:S(2)}) async-start(f32[4,72,128]{2,1,0:T(8,128)} %get-tuple-element.38), calls=%async_computation.1 | async-start | bytes 294912 | tf_op jit(solution)/shard_map/all_to_all | solution.py:536
  44.3 5.4 %all-to-all-done.1.got_ref = f32[4,72,128]{2,1,0:T(8,128)S(1)} async-done(((f32[4,72,128]{2,1,0:T(8,128)}), f32[4,72,128]{2,1,0:T(8,128)S(1)}, u32[]{:S(2)}, u32[]{:S(2)}) %all-to-all-start.1) | async-done | bytes 147488 | tf_op jit(solution)/shard_map/all_to_all | solution.py:536
  49.7 4.0 %collective-permute-start.2 = (f32[136,128]{1,0:T(8,128)S(1)}, f32[136,128]{1,0:T(8,128)S(1)}, u32[]{:S(2)}, u32[]{:S(2)}) collective-permute-start(f32[136,128]{1,0:T(8,128)S(1)} %get-tuple-element.41), channel_id=1, source_target_pairs={{0,9},{1,8},{2,11},{3,10},{4,13},{5,12},{6,15},{7,14},{8,17},{9,16... | collective-permute-start | bytes 208904 | tf_op jit(solution)/shard_map/ppermute | solution.py:538
  53.7 2.3 %collective-permute-start.1 = (f32[8,128]{1,0:T(8,128)S(1)}, f32[8,128]{1,0:T(8,128)S(1)}, u32[]{:S(2)}, u32[]{:S(2)}) collective-permute-start(f32[8,128]{1,0:T(8,128)S(1)} %get-tuple-element.40), channel_id=1, source_target_pairs={{0,8},{8,16},{16,24},{24,32},{32,40},{40,48},{48,56},{56,64},{64,7... | collective-permute-start | bytes 12296 | tf_op jit(solution)/shard_map/ppermute | solution.py:539
  56.0 0.6 shard_map.112
  56.6 6.0 %collective-permute-done.1.sum_ref = f32[8,128]{1,0:T(8,128)S(1)} collective-permute-done((f32[8,128]{1,0:T(8,128)S(1)}, f32[8,128]{1,0:T(8,128)S(1)}, u32[]{:S(2)}, u32[]{:S(2)}) %collective-permute-start.1) | collective-permute-done | bytes 4128 | tf_op jit(solution)/shard_map/ppermute | solution.py:539
  62.5 0.0 collective-permute-done.2.across_ref
  62.5 0.0 collective-permute-done.s2_ref
  62.5 0.0 copy-done
  62.5 3.0 %shard_map.113 = f32[512,512]{1,0:T(8,128)} custom-call(f32[512,512]{1,0:T(8,128)S(1)} %bitcast.6, f32[512,512]{1,0:T(8,128)S(1)} %collective-permute-done.s2_ref, f32[8,128]{1,0:T(8,128)S(1)} %collective-permute-done.1.sum_ref, f32[136,128]{1,0:T(8,128)S(1)} %collective-permute-done.2.across_ref, bf16[512,512]{1,0:T(8,128)(2,1)S(1)} %get-tuple-element.33.kh_ref, ...), custom_call_target="tpu_custom_call" | custom-call | flops 1000000000 | bytes 5496832 | tf_op jit(solution)/shard_map/pallas_call | solution.py:471
  (1 shorter events, 0.0 us)
Async XLA Ops:
  0.0 30.9 %copy-start.1 = (s32[256,8]{0,1:T(8,128)S(1)}, s32[256,8]{0,1:T(8,128)}, u32[]{:S(2)}) copy-start(s32[256,8]{0,1:T(8,128)} %param.16) | copy-start | bytes 24580
  0.0 30.9 %copy-start.2 = (f32[1,256,512]{2,1,0:T(8,128)S(1)}, f32[1,256,512]{2,1,0:T(8,128)}, u32[]{:S(2)}) copy-start(f32[1,256,512]{2,1,0:T(8,128)} %param.12) | copy-start | bytes 1572868
  0.0 30.9 %copy-start.3 = (f32[256,512]{1,0:T(8,128)S(1)}, f32[256,512]{1,0:T(8,128)}, u32[]{:S(2)}) copy-start(f32[256,512]{1,0:T(8,128)} %met_ref.1) | copy-start | bytes 1572868
  0.0 30.9 %copy-start.4 = (s32[256,6]{0,1:T(8,128)S(1)}, s32[256,6]{0,1:T(8,128)}, u32[]{:S(2)}) copy-start(s32[256,6]{0,1:T(8,128)} %param.15) | copy-start | bytes 18436
  0.0 30.9 %copy-start.5 = (bf16[512,256]{1,0:T(8,128)(2,1)S(1)}, bf16[512,256]{1,0:T(8,128)(2,1)}, u32[]{:S(2)}) copy-start(bf16[512,256]{1,0:T(8,128)(2,1)} %constant.8.clone.sel_hbm.sel_ref) | copy-start | bytes 786436
  0.0 30.9 %copy-start.6 = (f32[8,512]{1,0:T(8,128)S(1)}, f32[8,512]{1,0:T(8,128)}, u32[]{:S(2)}) copy-start(f32[8,512]{1,0:T(8,128)} %constant.6.clone.bas_hbm.bas_ref) | copy-start | bytes 49156
  0.0 30.9 %copy-start.7 = (f32[8,128]{1,0:T(8,128)S(1)}, f32[8,128]{1,0:T(8,128)}, u32[]{:S(2)}) copy-start(f32[8,128]{1,0:T(8,128)} %constant.7.clone.pair_hbm.pair_ref) | copy-start | bytes 12292
  38.2 24.3 %copy-start = (f32[1,2,256,512]{3,2,1,0:T(8,128)S(1)}, f32[1,2,256,512]{3,2,1,0:T(8,128)}, u32[]{:S(2)}) copy-start(f32[1,2,256,512]{3,2,1,0:T(8,128)} %param.11) | copy-start | bytes 3145732
  38.2 24.3 %collective-permute-start = (f32[512,512]{1,0:T(8,128)}, f32[512,512]{1,0:T(8,128)S(1)}, u32[]{:S(2)}, u32[]{:S(2)}) collective-permute-start(f32[512,512]{1,0:T(8,128)} %get-tuple-element.37), channel_id=1, source_target_pairs={{0,8},{8,16},{16,24},{24,32},{32,40},{40,48},{48,56},{56,64},{64,7... | collective-permute-start | bytes 3145736 | tf_op jit(solution)/shard_map/ppermute | solution.py:535
  40.3 9.4 %all-to-all-start.1 = ((f32[4,72,128]{2,1,0:T(8,128)}), f32[4,72,128]{2,1,0:T(8,128)S(1)}, u32[]{:S(2)}, u32[]{:S(2)}) async-start(f32[4,72,128]{2,1,0:T(8,128)} %get-tuple-element.38), calls=%async_computation.1 | async-start | bytes 294912 | tf_op jit(solution)/shard_map/all_to_all | solution.py:536
  49.7 12.8 %collective-permute-start.2 = (f32[136,128]{1,0:T(8,128)S(1)}, f32[136,128]{1,0:T(8,128)S(1)}, u32[]{:S(2)}, u32[]{:S(2)}) collective-permute-start(f32[136,128]{1,0:T(8,128)S(1)} %get-tuple-element.41), channel_id=1, source_target_pairs={{0,9},{1,8},{2,11},{3,10},{4,13},{5,12},{6,15},{7,14},{8,17},{9,16... | collective-permute-start | bytes 208904 | tf_op jit(solution)/shard_map/ppermute | solution.py:538
  53.7 8.8 %collective-permute-start.1 = (f32[8,128]{1,0:T(8,128)S(1)}, f32[8,128]{1,0:T(8,128)S(1)}, u32[]{:S(2)}, u32[]{:S(2)}) collective-permute-start(f32[8,128]{1,0:T(8,128)S(1)} %get-tuple-element.40), channel_id=1, source_target_pairs={{0,8},{8,16},{16,24},{24,32},{32,40},{40,48},{48,56},{56,64},{64,7... | collective-permute-start | bytes 12296 | tf_op jit(solution)/shard_map/ppermute | solution.py:539

commit v4 on v3

--- a/solution.py
+++ b/solution.py
@@ -279,8 +279,8 @@
 
 
 def first_kernel(
-    tan_hbm, swl_hbm, met_hbm, sti_hbm, fs_hbm, cor_hbm, sel_hbm, bas_hbm, pair_hbm, inv_hbm,
-    adv_ref, g_ref, msg_ref, p_ref, bm_ref, bh_ref, bl_ref, kh_ref, kl_ref, pl_ref, lb_ref,
+    tan_hbm, swl_hbm, met_hbm, sti_hbm, fs_hbm, cor_hbm, sel_hbm, bas_hbm, pair_hbm, inv_hbm, ang_ref,
+    adv_ref, g_ref, msg_ref, p_ref, bm_ref, bh_ref, bl_ref, kh_ref, kl_ref, pl_ref, lb_ref, turn_ref,
     q_ref, tan_ref, swl_ref, met_ref, sti_ref, fs_ref, cor_ref, sel_ref, bas_ref, pair_ref, inv_ref, sems,
 ):
     me = lax.axis_index("dom")
@@ -303,6 +303,10 @@
     ]
     for move in moves:
         move.start()
+    angle = jnp.where(lax.axis_index("seg") == 0, ang_ref[0], F32(0.0))
+    angles = jnp.full((8, 128), angle, F32)
+    turn_ref[0:8, :] = jnp.cos(angles)
+    turn_ref[8:16, :] = jnp.sin(angles)
     for move in moves[:3]:
         move.wait()
     bh, bl = split(stiff_matrix(sti_ref[...]))
@@ -424,11 +428,8 @@
     across_ref[8 + SHARED :, :] = got_ref[giver, 8:, :]
 
 
-def prepare_kernel(lb_ref, cor_ref, fs_ref, ang_ref, bm_ref, bas_ref, pl_ref, sel_ref, turn_ref):
-    angle = jnp.where(lax.axis_index("seg") == 0, ang_ref[0], F32(0.0))
-    angles = jnp.full((8, 128), angle, F32)
-    turn_ref[0:8, :] = jnp.cos(angles)
-    turn_ref[8:16, :] = jnp.sin(angles)
+def prepare_kernel(sum_ref, lb_ref, cor_ref, fs_ref, kept_ref, bm_ref, bas_ref, pl_ref, sel_ref):
+    kept_ref[...] = sum_ref[...]
     _, cvl = corner_parts(cor_ref)
     bm_ref[...] = hot(row_of(cvl) == iota((128, 1), 0).astype(F32))
     bas_ref[...] = lb_ref[:, :NODES]
@@ -496,7 +497,7 @@
     faces = pltpu.VMEM((count, 2 * HALO), BF16)
 
     ins = [state, swirl, metric, stiffness, slots, ids, select, basis, pair, coarse_inverse]
-    advanced, g, msg, p, bm, bh, bl, kh, kl, placed, lb = call(
+    advanced, g, msg, p, bm, bh, bl, kh, kl, placed, lb, turn = call(
         first_kernel,
         [
             field,
@@ -510,13 +511,14 @@
             square,
             like(count, HALO, dtype=BF16),
             like(32, 2 * NODES, dtype=BF16),
+            like(16, 128),
         ],
         [faces]
         + [pltpu.VMEM(a.shape, a.dtype) for a in ins]
         + [pltpu.SemaphoreType.DMA((len(ins),))],
-        [pltpu.with_memory_space_constraint(a, pltpu.HBM) for a in ins],
+        [pltpu.with_memory_space_constraint(a, pltpu.HBM) for a in ins] + [phase_angle],
         4_000_000_000,
-        [HBM] * len(ins),
+        [HBM] * len(ins) + [pl.BlockSpec(memory_space=pltpu.SMEM)],
     )
     got = lax.all_to_all(msg, "dom", 0, 0)
     s2, msg, near = call(
@@ -536,21 +538,20 @@
     got = lax.all_to_all(msg, "dom", 0, 0, axis_index_groups=[[0, 2, 4, 6], [1, 3, 5, 7]])
     total, across = call(pack_kernel, [like(8, 128), like(8 + HALO, 128)], [], [got, near], 1_000_000)
     across = lax.ppermute(across, ("seg", "dom"), onward(lambda d: d ^ 1))
-    total = lax.ppermute(total, "seg", ring)
-    bm, wide, placed, select, turn = call(
+    total, bm, wide, placed, select = call(
         prepare_kernel,
         [
+            like(8, 128),
             like(128, 8 * ELEMS, dtype=BF16),
             like(32, NODES, dtype=BF16),
             like(count, HALO, dtype=BF16),
             like(NODES, 4 * PLANE, dtype=BF16),
-            like(16, 128),
         ],
         [],
-        [lb, ids, slots, phase_angle],
+        [total, lb, ids, slots],
         1_000_000_000,
-        [VMEM] * 3 + [pl.BlockSpec(memory_space=pltpu.SMEM)],
     )
+    total = lax.ppermute(total, "seg", ring)
     (out,) = call(
         last_kernel,
         [field],

time: 65.9 us -> 65.5 us (level)
  blocking collectives: 23.6 us -> 32.1 us
  waiting for transfers between devices: 11.3 us -> 6.52 us
  starting transfers between devices: 11.7 us -> 8.35 us
    all_to_all x0 -> x1, blocking collectives: none -> 8.41 us  [shards(): lax.all_to_all(msg, 'dom', 0, 0, axis_index_groups=[[0, 2, 4, 6], [1, 3,...]
    all_to_all x1 -> x0, waiting for transfers between devices: 5.38 us -> none  [shards(): lax.all_to_all(msg, 'dom', 0, 0, axis_index_groups=[[0, 2, 4, 6], [1, 3,...]
    all_to_all x1 -> x0, starting transfers between devices: 3.35 us -> none  [shards(): lax.all_to_all(msg, 'dom', 0, 0, axis_index_groups=[[0, 2, 4, 6], [1, 3,...]
  transfers between devices with their start and end apart: 4 -> 3, of which waited for: 2 -> 1; matrix products, arithmetic and copies ran while one was open for 0% -> 0% of each run, Pallas kernels for 1% -> 1%
where the time goes in v4:
time: 65.5 us; the launch traced here: 65.2 us
  blocking collectives  32.1 us (49%)
  Pallas kernels  17.5 us (27%)
  starting transfers between devices  8.35 us (13%)
  waiting for transfers between devices  6.52 us (10%)
  between operations  0.79 us (1%)
    all_to_all x1, blocking collectives, shards(): got = lax.all_to_all(msg, 'dom', 0, 0)  23.6 us
    pallas_call x5, Pallas kernels, call(): pl.pallas_call(body, out_shape=outs, in_specs=specs or [VMEM] * len(ins),...  17.5 us
    all_to_all x1, blocking collectives, shards(): lax.all_to_all(msg, 'dom', 0, 0, axis_index_groups=[[0, 2, 4, 6], [1, 3,...  8.41 us
    ppermute x1, waiting for transfers between devices, shards(): total = lax.ppermute(total, 'seg', ring)  6.52 us
    ppermute x1, starting transfers between devices, shards(): across = lax.ppermute(across, ('seg', 'dom'), onward(lambda d: d ^ 1))  3.97 us
    ppermute x1, starting transfers between devices, shards(): total = lax.ppermute(total, 'seg', ring)  2.31 us
    ppermute x1, starting transfers between devices, shards(): s2 = lax.ppermute(s2, 'seg', ring)  2.06 us
  transfers between devices with their start and end apart: 3, of which 1 were waited for; matrix products, arithmetic and copies ran while one was open for 0% of the time, Pallas kernels for 1%

profile of v4, /device:TPU:256, one launch (start us, length us, event | category | flops | bytes accessed | tf_op | source)
XLA Modules:
  0.0 65.2 jit_solution(17791978252291106445)
XLA Ops:
  0.7 0.0 copy-start.1
  0.7 0.0 copy-start.2
  0.7 0.0 copy-start.3
  0.7 0.0 copy-start.4
  0.7 0.0 copy-start.5
  0.7 0.0 copy-start.6
  0.7 0.0 copy-start.7
  0.7 7.2 %shard_map.109 = (f32[512,512]{1,0:T(8,128)S(1)}, bf16[1536,256]{1,0:T(8,128)(2,1)S(1)}, f32[8,88,128]{2,1,0:T(8,128)S(1)}, bf16[1536,1536]{1,0:T(8,128)(2,1)S(1...) custom-call(f32[512,512]{1,0:T(8,128)} %bitcast.5, ...), custom_call_target="tpu_custom_call" | custom-call | flops 4000000000 | bytes 13445380 | tf_op jit(solution)/shard_map/pallas_call | solution.py:472
  7.9 23.6 %all_to_all.10.got_ref = f32[8,88,128]{2,1,0:T(8,128)S(1)} all-to-all(f32[8,88,128]{2,1,0:T(8,128)S(1)} %get-tuple-element.29), channel_id=1, replica_groups=mesh['seg'=64,'dom'=8] {'dom'}, dimensions={0} | all-to-all | bytes 720896 | tf_op jit(solution)/shard_map/all_to_all | solution.py:523
  31.6 0.0 copy-done.1
  31.6 0.0 copy-done.2
  31.6 0.0 copy-done.3
  31.6 0.0 copy-done.4
  31.6 0.0 copy-done.5
  31.6 0.0 copy-done.6
  31.6 0.0 copy-done.7
  31.6 6.6 %shard_map.110 = (f32[512,512]{1,0:T(8,128)S(1)}, f32[4,72,128]{2,1,0:T(8,128)S(1)}, f32[64,128]{1,0:T(8,128)S(1)}) custom-call(f32[512,512]{1,0:T(8,128)S(1)} %get-tuple-element.27.adv_ref, bf16[1536,256]{1,0:T(8,128)(2,1)S(1)} %get-tuple-element.28.g1_ref, f32[8,88,128]{2,1,0:T(8,128)S(1)} %all_to_all.10.got_ref, ...), custom_call_target="tpu_custom_call" | custom-call | flops 4000000000 | bytes 12568576 | tf_op jit(solution)/shard_map/pallas_call | solution.py:472
  38.2 0.0 copy-start
  38.2 2.1 %collective-permute-start = (f32[512,512]{1,0:T(8,128)S(1)}, f32[512,512]{1,0:T(8,128)S(1)}, u32[]{:S(2)}, u32[]{:S(2)}) collective-permute-start(f32[512,512]{1,0:T(8,128)S(1)} %get-tuple-element.38), channel_id=1, source_target_pairs={{0,8},{8,16},{16,24},{24,32},{32,40},{40,48},{48,56},{56,64},{64,7... | collective-permute-start | bytes 3145736 | tf_op jit(solution)/shard_map/ppermute | solution.py:537
  40.3 8.4 %all_to_all.11.got_ref = f32[4,72,128]{2,1,0:T(8,128)S(1)} all-to-all(f32[4,72,128]{2,1,0:T(8,128)S(1)} %get-tuple-element.39), channel_id=1, replica_groups={{0,2,4,6},{1,3,5,7},{8,10,12,14},{9,11,13,15},{16,18,20,22},{17,19,21,2..., dimensions={0} | all-to-all | bytes 294912 | tf_op jit(solution)/shard_map/all_to_all | solution.py:538
  48.7 4.0 %collective-permute-start.2 = (f32[136,128]{1,0:T(8,128)S(1)}, f32[136,128]{1,0:T(8,128)S(1)}, u32[]{:S(2)}, u32[]{:S(2)}) collective-permute-start(f32[136,128]{1,0:T(8,128)S(1)} %get-tuple-element.43), channel_id=1, source_target_pairs={{0,9},{1,8},{2,11},{3,10},{4,13},{5,12},{6,15},{7,14},{8,17},{9,16... | collective-permute-start | bytes 208904 | tf_op jit(solution)/shard_map/ppermute | solution.py:540
  52.7 0.6 shard_map.112
  53.3 2.3 %collective-permute-start.1 = (f32[8,128]{1,0:T(8,128)S(1)}, f32[8,128]{1,0:T(8,128)S(1)}, u32[]{:S(2)}, u32[]{:S(2)}) collective-permute-start(f32[8,128]{1,0:T(8,128)S(1)} %get-tuple-element.42), channel_id=1, source_target_pairs={{0,8},{8,16},{16,24},{24,32},{32,40},{40,48},{48,56},{56,64},{64,7... | collective-permute-start | bytes 12296 | tf_op jit(solution)/shard_map/ppermute | solution.py:554
  55.6 6.5 %collective-permute-done.1.sum_ref = f32[8,128]{1,0:T(8,128)S(1)} collective-permute-done((f32[8,128]{1,0:T(8,128)S(1)}, f32[8,128]{1,0:T(8,128)S(1)}, u32[]{:S(2)}, u32[]{:S(2)}) %collective-permute-start.1) | collective-permute-done | bytes 4128 | tf_op jit(solution)/shard_map/ppermute | solution.py:554
  62.1 0.0 collective-permute-done.2.across_ref
  62.1 0.0 collective-permute-done.s2_ref
  62.1 0.0 copy-done
  62.1 3.1 %shard_map.113 = f32[512,512]{1,0:T(8,128)} custom-call(f32[512,512]{1,0:T(8,128)S(1)} %bitcast.6, f32[512,512]{1,0:T(8,128)S(1)} %collective-permute-done.s2_ref, f32[8,128]{1,0:T(8,128)S(1)} %collective-permute-done.1.sum_ref, f32[136,128]{1,0:T(8,128)S(1)} %collective-permute-done.2.across_ref, bf16[512,512]{1,0:T(8,128)(2,1)S(1)} %get-tuple-element.34.kh_ref, ...), custom_call_target="tpu_custom_call" | custom-call | flops 1000000000 | bytes 5496832 | tf_op jit(solution)/shard_map/pallas_call | solution.py:472
  (1 shorter events, 0.0 us)
Async XLA Ops:
  0.7 30.9 %copy-start.1 = (s32[256,8]{0,1:T(8,128)S(1)}, s32[256,8]{0,1:T(8,128)}, u32[]{:S(2)}) copy-start(s32[256,8]{0,1:T(8,128)} %param.16) | copy-start | bytes 24580
  0.7 30.9 %copy-start.2 = (f32[1,256,512]{2,1,0:T(8,128)S(1)}, f32[1,256,512]{2,1,0:T(8,128)}, u32[]{:S(2)}) copy-start(f32[1,256,512]{2,1,0:T(8,128)} %param.12) | copy-start | bytes 1572868
  0.7 30.9 %copy-start.3 = (f32[256,512]{1,0:T(8,128)S(1)}, f32[256,512]{1,0:T(8,128)}, u32[]{:S(2)}) copy-start(f32[256,512]{1,0:T(8,128)} %met_ref.1) | copy-start | bytes 1572868
  0.7 30.9 %copy-start.4 = (s32[256,6]{0,1:T(8,128)S(1)}, s32[256,6]{0,1:T(8,128)}, u32[]{:S(2)}) copy-start(s32[256,6]{0,1:T(8,128)} %param.15) | copy-start | bytes 18436
  0.7 30.9 %copy-start.5 = (bf16[512,256]{1,0:T(8,128)(2,1)S(1)}, bf16[512,256]{1,0:T(8,128)(2,1)}, u32[]{:S(2)}) copy-start(bf16[512,256]{1,0:T(8,128)(2,1)} %constant.8.clone.sel_hbm.sel_ref) | copy-start | bytes 786436
  0.7 30.9 %copy-start.6 = (f32[8,512]{1,0:T(8,128)S(1)}, f32[8,512]{1,0:T(8,128)}, u32[]{:S(2)}) copy-start(f32[8,512]{1,0:T(8,128)} %constant.6.clone.bas_hbm.bas_ref) | copy-start | bytes 49156
  0.7 30.9 %copy-start.7 = (f32[8,128]{1,0:T(8,128)S(1)}, f32[8,128]{1,0:T(8,128)}, u32[]{:S(2)}) copy-start(f32[8,128]{1,0:T(8,128)} %constant.7.clone.pair_hbm.pair_ref) | copy-start | bytes 12292
  38.2 23.9 %copy-start = (f32[1,2,256,512]{3,2,1,0:T(8,128)S(1)}, f32[1,2,256,512]{3,2,1,0:T(8,128)}, u32[]{:S(2)}) copy-start(f32[1,2,256,512]{3,2,1,0:T(8,128)} %param.11) | copy-start | bytes 3145732
  38.2 23.9 %collective-permute-start = (f32[512,512]{1,0:T(8,128)S(1)}, f32[512,512]{1,0:T(8,128)S(1)}, u32[]{:S(2)}, u32[]{:S(2)}) collective-permute-start(f32[512,512]{1,0:T(8,128)S(1)} %get-tuple-element.38), channel_id=1, source_target_pairs={{0,8},{8,16},{16,24},{24,32},{32,40},{40,48},{48,56},{56,64},{64,7... | collective-permute-start | bytes 3145736 | tf_op jit(solution)/shard_map/ppermute | solution.py:537
  48.7 13.4 %collective-permute-start.2 = (f32[136,128]{1,0:T(8,128)S(1)}, f32[136,128]{1,0:T(8,128)S(1)}, u32[]{:S(2)}, u32[]{:S(2)}) collective-permute-start(f32[136,128]{1,0:T(8,128)S(1)} %get-tuple-element.43), channel_id=1, source_target_pairs={{0,9},{1,8},{2,11},{3,10},{4,13},{5,12},{6,15},{7,14},{8,17},{9,16... | collective-permute-start | bytes 208904 | tf_op jit(solution)/shard_map/ppermute | solution.py:540
  53.3 8.8 %collective-permute-start.1 = (f32[8,128]{1,0:T(8,128)S(1)}, f32[8,128]{1,0:T(8,128)S(1)}, u32[]{:S(2)}, u32[]{:S(2)}) collective-permute-start(f32[8,128]{1,0:T(8,128)S(1)} %get-tuple-element.42), channel_id=1, source_target_pairs={{0,8},{8,16},{16,24},{24,32},{32,40},{40,48},{48,56},{56,64},{64,7... | collective-permute-start | bytes 12296 | tf_op jit(solution)/shard_map/ppermute | solution.py:554

commit v5 on v4

--- a/solution.py
+++ b/solution.py
@@ -280,7 +280,7 @@
 
 def first_kernel(
     tan_hbm, swl_hbm, met_hbm, sti_hbm, fs_hbm, cor_hbm, sel_hbm, bas_hbm, pair_hbm, inv_hbm, ang_ref,
-    adv_ref, g_ref, msg_ref, p_ref, bm_ref, bh_ref, bl_ref, kh_ref, kl_ref, pl_ref, lb_ref, turn_ref,
+    adv_ref, g_ref, msg_ref, p_ref, bm_ref, bh_ref, bl_ref, kh_ref, kl_ref, pl_ref, turn_ref,
     q_ref, tan_ref, swl_ref, met_ref, sti_ref, fs_ref, cor_ref, sel_ref, bas_ref, pair_ref, inv_ref, sems,
 ):
     me = lax.axis_index("dom")
@@ -341,10 +341,6 @@
         pl_ref[f * ELEMS : (f + 1) * ELEMS, :] = hot(columns[f] == target)
     for move in moves[3:9]:
         move.wait()
-    basis = bas_ref[...]
-    stiff = stiff_of(jnp.concatenate([basis, basis], axis=0), bh_ref[...], bl_ref[...])
-    lb_ref[:, :NODES] = tripled(basis)
-    lb_ref[:, NODES:] = tripled(stiff[:8])
 
     state = tan_ref[...]
     advanced = advance(state, stiff_of(state, bh_ref[...], bl_ref[...]), met_ref[...], swl_ref[...])
@@ -363,7 +359,7 @@
 
 
 def second_kernel(
-    adv_ref, g1_ref, got_ref, p_ref, bm_ref, bh_ref, bl_ref, kh_ref, kl_ref, pl_ref, lb_ref, swl_ref, met_ref, fs_ref, cor_ref,
+    adv_ref, g1_ref, got_ref, p_ref, bm_ref, bh_ref, bl_ref, kh_ref, kl_ref, pl_ref, swl_ref, met_ref, fs_ref, cor_ref,
     sel_ref, bas_ref, pair_ref,
     out_ref, msg_ref, near_ref, q_ref, g_ref,
 ):
@@ -377,7 +373,10 @@
     arrived = jnp.concatenate([got_ref[before, 24:MSG1, :], got_ref[after, 24:MSG1, :]], axis=0)
     partner = g1_ref[...].astype(F32) + halo_faces(pl_ref[...], arrived)
     partly = settle(adv_ref[...], partner, select)
-    stiff = stiff_of(partly, bh_ref[...], bl_ref[...])
+    basis = bas_ref[...]
+    stiff = stiff_of(jnp.concatenate([partly, basis, basis], axis=0), bh_ref[...], bl_ref[...])
+    wide = jnp.concatenate([tripled(basis), tripled(stiff[2 * ELEMS : 2 * ELEMS + 8])], axis=1)
+    stiff = stiff[: 2 * ELEMS]
 
     coarse = got_ref[0, 0:8, :]
     for j in range(1, 8):
@@ -393,7 +392,7 @@
             eight(rf[r : r + 1, :], rf[4 + r : 5 + r, :]), partner[r : r + 1, :], low_hot
         )
     solved = solve(coarse, kh_ref[...], kl_ref[...])
-    both = dot_tn(corner_values(solved, cvh_row, bm_ref[...]), lb_ref[...])
+    both = dot_tn(corner_values(solved, cvh_row, bm_ref[...]), wide)
     advanced = advance(partly - both[:, :NODES], stiff - both[:, NODES:], met_ref[...], swl_ref[...])
     blocks, ah, al = face_blocks(advanced, select)
     pair_up(blocks, p_ref, q_ref, g_ref)
@@ -428,11 +427,11 @@
     across_ref[8 + SHARED :, :] = got_ref[giver, 8:, :]
 
 
-def prepare_kernel(sum_ref, lb_ref, cor_ref, fs_ref, kept_ref, bm_ref, bas_ref, pl_ref, sel_ref):
+def prepare_kernel(sum_ref, basis_ref, cor_ref, fs_ref, kept_ref, bm_ref, bas_ref, pl_ref, sel_ref):
     kept_ref[...] = sum_ref[...]
     _, cvl = corner_parts(cor_ref)
     bm_ref[...] = hot(row_of(cvl) == iota((128, 1), 0).astype(F32))
-    bas_ref[...] = lb_ref[:, :NODES]
+    bas_ref[...] = tripled(basis_ref[...])
     columns = slot_columns(fs_ref)
     target = shared_target_row()
     for f in range(FACES):
@@ -497,7 +496,7 @@
     faces = pltpu.VMEM((count, 2 * HALO), BF16)
 
     ins = [state, swirl, metric, stiffness, slots, ids, select, basis, pair, coarse_inverse]
-    advanced, g, msg, p, bm, bh, bl, kh, kl, placed, lb, turn = call(
+    advanced, g, msg, p, bm, bh, bl, kh, kl, placed, turn = call(
         first_kernel,
         [
             field,
@@ -510,7 +509,6 @@
             square,
             square,
             like(count, HALO, dtype=BF16),
-            like(32, 2 * NODES, dtype=BF16),
             like(16, 128),
         ],
         [faces]
@@ -525,7 +523,7 @@
         second_kernel,
         [field, like(4, 8 + SHARED, 128), like(SHARED, 128)],
         [faces, faces],
-        [advanced, g, got, p, bm, bh, bl, kh, kl, placed, lb, swirl, metric, slots, ids, select, basis, pair],
+        [advanced, g, got, p, bm, bh, bl, kh, kl, placed, swirl, metric, slots, ids, select, basis, pair],
         4_000_000_000,
     )
     size = lax.axis_size("seg")
@@ -548,7 +546,7 @@
             like(NODES, 4 * PLANE, dtype=BF16),
         ],
         [],
-        [total, lb, ids, slots],
+        [total, basis, ids, slots],
         1_000_000_000,
     )
     total = lax.ppermute(total, "seg", ring)

time: 65.5 us -> 65.1 us (level)
  no operation moved by 1% of the time
where the time goes in v5:
time: 65.1 us; the launch traced here: 64.8 us
  blocking collectives  32.1 us (49%)
  Pallas kernels  17.1 us (26%)
  starting transfers between devices  8.34 us (13%)
  waiting for transfers between devices  6.52 us (10%)
  between operations  0.79 us (1%)
    all_to_all x1, blocking collectives, shards(): got = lax.all_to_all(msg, 'dom', 0, 0)  23.6 us
    pallas_call x5, Pallas kernels, call(): pl.pallas_call(body, out_shape=outs, in_specs=specs or [VMEM] * len(ins),...  17.1 us
    all_to_all x1, blocking collectives, shards(): lax.all_to_all(msg, 'dom', 0, 0, axis_index_groups=[[0, 2, 4, 6], [1, 3,...  8.41 us
    ppermute x1, waiting for transfers between devices, shards(): total = lax.ppermute(total, 'seg', ring)  6.52 us
    ppermute x1, starting transfers between devices, shards(): across = lax.ppermute(across, ('seg', 'dom'), onward(lambda d: d ^ 1))  3.97 us
    ppermute x1, starting transfers between devices, shards(): total = lax.ppermute(total, 'seg', ring)  2.31 us
    ppermute x1, starting transfers between devices, shards(): s2 = lax.ppermute(s2, 'seg', ring)  2.06 us
  transfers between devices with their start and end apart: 3, of which 1 were waited for; matrix products, arithmetic and copies ran while one was open for 0% of the time, Pallas kernels for 1%

profile of v5, /device:TPU:256, one launch (start us, length us, event | category | flops | bytes accessed | tf_op | source)
XLA Modules:
  0.0 64.8 jit_solution(6475579985355501521)
XLA Ops:
  0.7 0.0 copy-start.1
  0.7 0.0 copy-start.2
  0.7 0.0 copy-start.3
  0.7 0.0 copy-start.4
  0.7 0.0 copy-start.5
  0.7 0.0 copy-start.6
  0.7 0.0 copy-start.7
  0.7 6.7 %shard_map.109 = (f32[512,512]{1,0:T(8,128)S(1)}, bf16[1536,256]{1,0:T(8,128)(2,1)S(1)}, f32[8,88,128]{2,1,0:T(8,128)S(1)}, bf16[1536,1536]{1,0:T(8,128)(2,1)S(1...) custom-call(f32[512,512]{1,0:T(8,128)} %bitcast.5, ...), custom_call_target="tpu_custom_call" | custom-call | flops 4000000000 | bytes 13379844 | tf_op jit(solution)/shard_map/pallas_call | solution.py:471
  7.5 23.6 %all_to_all.10.got_ref = f32[8,88,128]{2,1,0:T(8,128)S(1)} all-to-all(f32[8,88,128]{2,1,0:T(8,128)S(1)} %get-tuple-element.28), channel_id=1, replica_groups=mesh['seg'=64,'dom'=8] {'dom'}, dimensions={0} | all-to-all | bytes 720896 | tf_op jit(solution)/shard_map/all_to_all | solution.py:521
  31.1 0.0 copy-done.1
  31.1 0.0 copy-done.2
  31.1 0.0 copy-done.3
  31.1 0.0 copy-done.4
  31.1 0.0 copy-done.5
  31.2 0.0 copy-done.6
  31.2 0.0 copy-done.7
  31.2 6.6 %shard_map.110 = (f32[512,512]{1,0:T(8,128)S(1)}, f32[4,72,128]{2,1,0:T(8,128)S(1)}, f32[64,128]{1,0:T(8,128)S(1)}) custom-call(f32[512,512]{1,0:T(8,128)S(1)} %get-tuple-element.26.adv_ref, bf16[1536,256]{1,0:T(8,128)(2,1)S(1)} %get-tuple-element.27.g1_ref, f32[8,88,128]{2,1,0:T(8,128)S(1)} %all_to_all.10.got_ref, ...), custom_call_target="tpu_custom_call" | custom-call | flops 4000000000 | bytes 12503040 | tf_op jit(solution)/shard_map/pallas_call | solution.py:471
  37.8 0.0 copy-start
  37.8 2.1 %collective-permute-start = (f32[512,512]{1,0:T(8,128)S(1)}, f32[512,512]{1,0:T(8,128)S(1)}, u32[]{:S(2)}, u32[]{:S(2)}) collective-permute-start(f32[512,512]{1,0:T(8,128)S(1)} %get-tuple-element.36), channel_id=1, source_target_pairs={{0,8},{8,16},{16,24},{24,32},{32,40},{40,48},{48,56},{56,64},{64,7... | collective-permute-start | bytes 3145736 | tf_op jit(solution)/shard_map/ppermute | solution.py:535
  39.9 8.4 %all_to_all.11.got_ref = f32[4,72,128]{2,1,0:T(8,128)S(1)} all-to-all(f32[4,72,128]{2,1,0:T(8,128)S(1)} %get-tuple-element.37), channel_id=1, replica_groups={{0,2,4,6},{1,3,5,7},{8,10,12,14},{9,11,13,15},{16,18,20,22},{17,19,21,2..., dimensions={0} | all-to-all | bytes 294912 | tf_op jit(solution)/shard_map/all_to_all | solution.py:536
  48.3 4.0 %collective-permute-start.2 = (f32[136,128]{1,0:T(8,128)S(1)}, f32[136,128]{1,0:T(8,128)S(1)}, u32[]{:S(2)}, u32[]{:S(2)}) collective-permute-start(f32[136,128]{1,0:T(8,128)S(1)} %get-tuple-element.41), channel_id=1, source_target_pairs={{0,9},{1,8},{2,11},{3,10},{4,13},{5,12},{6,15},{7,14},{8,17},{9,16... | collective-permute-start | bytes 208904 | tf_op jit(solution)/shard_map/ppermute | solution.py:538
  52.3 0.6 shard_map.112
  52.9 2.3 %collective-permute-start.1 = (f32[8,128]{1,0:T(8,128)S(1)}, f32[8,128]{1,0:T(8,128)S(1)}, u32[]{:S(2)}, u32[]{:S(2)}) collective-permute-start(f32[8,128]{1,0:T(8,128)S(1)} %get-tuple-element.40), channel_id=1, source_target_pairs={{0,8},{8,16},{16,24},{24,32},{32,40},{40,48},{48,56},{56,64},{64,7... | collective-permute-start | bytes 12296 | tf_op jit(solution)/shard_map/ppermute | solution.py:552
  55.2 6.5 %collective-permute-done.1.sum_ref = f32[8,128]{1,0:T(8,128)S(1)} collective-permute-done((f32[8,128]{1,0:T(8,128)S(1)}, f32[8,128]{1,0:T(8,128)S(1)}, u32[]{:S(2)}, u32[]{:S(2)}) %collective-permute-start.1) | collective-permute-done | bytes 4128 | tf_op jit(solution)/shard_map/ppermute | solution.py:552
  61.7 0.0 collective-permute-done.2.across_ref
  61.7 0.0 collective-permute-done.s2_ref
  61.7 0.0 copy-done
  61.7 3.1 %shard_map.113 = f32[512,512]{1,0:T(8,128)} custom-call(f32[512,512]{1,0:T(8,128)S(1)} %bitcast.6, f32[512,512]{1,0:T(8,128)S(1)} %collective-permute-done.s2_ref, f32[8,128]{1,0:T(8,128)S(1)} %collective-permute-done.1.sum_ref, f32[136,128]{1,0:T(8,128)S(1)} %collective-permute-done.2.across_ref, bf16[512,512]{1,0:T(8,128)(2,1)S(1)} %get-tuple-element.33.kh_ref, ...), custom_call_target="tpu_custom_call" | custom-call | flops 1000000000 | bytes 5496832 | tf_op jit(solution)/shard_map/pallas_call | solution.py:471
  (1 shorter events, 0.0 us)
Async XLA Ops:
  0.7 30.5 %copy-start.1 = (s32[256,8]{0,1:T(8,128)S(1)}, s32[256,8]{0,1:T(8,128)}, u32[]{:S(2)}) copy-start(s32[256,8]{0,1:T(8,128)} %param.16) | copy-start | bytes 24580
  0.7 30.5 %copy-start.2 = (f32[1,256,512]{2,1,0:T(8,128)S(1)}, f32[1,256,512]{2,1,0:T(8,128)}, u32[]{:S(2)}) copy-start(f32[1,256,512]{2,1,0:T(8,128)} %param.12) | copy-start | bytes 1572868
  0.7 30.5 %copy-start.3 = (f32[256,512]{1,0:T(8,128)S(1)}, f32[256,512]{1,0:T(8,128)}, u32[]{:S(2)}) copy-start(f32[256,512]{1,0:T(8,128)} %met_ref.1) | copy-start | bytes 1572868
  0.7 30.5 %copy-start.4 = (s32[256,6]{0,1:T(8,128)S(1)}, s32[256,6]{0,1:T(8,128)}, u32[]{:S(2)}) copy-start(s32[256,6]{0,1:T(8,128)} %param.15) | copy-start | bytes 18436
  0.7 30.5 %copy-start.5 = (bf16[512,256]{1,0:T(8,128)(2,1)S(1)}, bf16[512,256]{1,0:T(8,128)(2,1)}, u32[]{:S(2)}) copy-start(bf16[512,256]{1,0:T(8,128)(2,1)} %constant.8.clone.sel_hbm.sel_ref) | copy-start | bytes 786436
  0.7 30.4 %copy-start.6 = (f32[8,512]{1,0:T(8,128)S(1)}, f32[8,512]{1,0:T(8,128)}, u32[]{:S(2)}) copy-start(f32[8,512]{1,0:T(8,128)} %constant.6.clone.bas_hbm.bas_ref.basis_ref) | copy-start | bytes 49156
  0.7 30.4 %copy-start.7 = (f32[8,128]{1,0:T(8,128)S(1)}, f32[8,128]{1,0:T(8,128)}, u32[]{:S(2)}) copy-start(f32[8,128]{1,0:T(8,128)} %constant.7.clone.pair_hbm.pair_ref) | copy-start | bytes 12292
  37.8 23.9 %copy-start = (f32[1,2,256,512]{3,2,1,0:T(8,128)S(1)}, f32[1,2,256,512]{3,2,1,0:T(8,128)}, u32[]{:S(2)}) copy-start(f32[1,2,256,512]{3,2,1,0:T(8,128)} %param.11) | copy-start | bytes 3145732
  37.8 23.9 %collective-permute-start = (f32[512,512]{1,0:T(8,128)S(1)}, f32[512,512]{1,0:T(8,128)S(1)}, u32[]{:S(2)}, u32[]{:S(2)}) collective-permute-start(f32[512,512]{1,0:T(8,128)S(1)} %get-tuple-element.36), channel_id=1, source_target_pairs={{0,8},{8,16},{16,24},{24,32},{32,40},{40,48},{48,56},{56,64},{64,7... | collective-permute-start | bytes 3145736 | tf_op jit(solution)/shard_map/ppermute | solution.py:535
  48.3 13.4 %collective-permute-start.2 = (f32[136,128]{1,0:T(8,128)S(1)}, f32[136,128]{1,0:T(8,128)S(1)}, u32[]{:S(2)}, u32[]{:S(2)}) collective-permute-start(f32[136,128]{1,0:T(8,128)S(1)} %get-tuple-element.41), channel_id=1, source_target_pairs={{0,9},{1,8},{2,11},{3,10},{4,13},{5,12},{6,15},{7,14},{8,17},{9,16... | collective-permute-start | bytes 208904 | tf_op jit(solution)/shard_map/ppermute | solution.py:538
  52.9 8.8 %collective-permute-start.1 = (f32[8,128]{1,0:T(8,128)S(1)}, f32[8,128]{1,0:T(8,128)S(1)}, u32[]{:S(2)}, u32[]{:S(2)}) collective-permute-start(f32[8,128]{1,0:T(8,128)S(1)} %get-tuple-element.40), channel_id=1, source_target_pairs={{0,8},{8,16},{16,24},{24,32},{32,40},{40,48},{48,56},{56,64},{64,7... | collective-permute-start | bytes 12296 | tf_op jit(solution)/shard_map/ppermute | solution.py:552
